TPU v7x, 32 devices: a whole 2x2x4 slice. The times are simulated.
32 devices in a mesh: section: 2 (over y), ctx: 4 (over z), tp: 4 (over x, core).
Axes of the slice: x: 2, y: 2, z: 4, core: 2. Of those that a mesh axis runs over, the one named last changes fastest.
Arguments:
- section_input: bfloat16 [4, 4096, 768], P(None, 'ctx'), may hold values from -6 to 6
- cotangent: bfloat16 [4, 4096, 768], P(None, 'ctx'), may hold values from -6 to 6
- counts: int32 [4, 4], replicated, may hold values from 256 to 1024, as said below
- norm_gain: bfloat16 [2, 2, 768], P('section', None, 'ctx'), may hold values from 0.5 to 1.5
- vector_bias: bfloat16 [2, 4, 768], P('section', None, 'ctx'), may hold values from -4 to 4
- qkv_weight: bfloat16 [2, 3, 768, 768], P('section', None, 'ctx', 'tp'), may hold values from -0.21875 to 0.21875
- head_bias: bfloat16 [2, 2, 12, 64], P('section', None, 'tp', 'ctx'), may hold values from -0.3125 to 0.3125
- out_weight: bfloat16 [2, 768, 768], P('section', 'tp', 'ctx'), may hold values from -6 to 6
- up_weight: bfloat16 [2, 768, 3072], P('section', 'ctx', 'tp'), may hold values from -0.21875 to 0.21875
- up_bias: bfloat16 [2, 48, 64], P('section', 'tp', 'ctx'), may hold values from -4 to 4
- down_weight: bfloat16 [2, 3072, 768], P('section', 'tp', 'ctx'), may hold values from -0.109375 to 0.109375
Outputs:
- acts: bfloat16 [2, 4, 4096, 768], P('section', None, 'ctx')
- in_grads: bfloat16 [2, 4, 4096, 768], P('section', None, 'ctx')
- grad_norm_gain: float32 [2, 2, 768], P('section', None, 'ctx')
- grad_vector_bias: float32 [2, 4, 768], P('section', None, 'ctx')
- grad_qkv: float32 [2, 3, 768, 768], P('section', None, 'ctx', 'tp')
- grad_head_bias: float32 [2, 2, 12, 64], P('section', None, 'tp', 'ctx')
- grad_out: float32 [2, 768, 768], P('section', 'tp', 'ctx')
- grad_up: float32 [2, 768, 3072], P('section', 'ctx', 'tp')
- grad_up_bias: float32 [2, 48, 64], P('section', 'tp', 'ctx')
- grad_down: float32 [2, 3072, 768], P('section', 'tp', 'ctx')
Inputs may be any that keep to these rules, and one draw needn't show every extreme that they name: counts[m, i] is the number of live rows of device i of ctx in micro-batch m: its first counts[m, i] row slots hold tokens, the others are padding. Each row of counts sums to 2048, and its largest entry is 1024.
All inputs are finite; a program needn't handle non-finite values.
Results may differ from a plain program's by a relative error of at most 0.025.
Values may be sent and summed in bfloat16 or wider, within the bound.
A program may use at most 320 MiB of HBM per device.

v0:
```python
from functools import partial
import math

import jax
import jax.numpy as jnp
from jax import lax
from jax.sharding import PartitionSpec as P

HD = 64


EPSILON = 1e-06
NEGATIVE_FILL = -1e30


def from_behind(block, axis, distance):
    devices = range(lax.axis_size(axis))
    route = [(i - distance, i) for i in devices if i - distance in devices]
    return lax.ppermute(block, axis, route)


def product(left, right):
    return jnp.dot(left, right, preferred_element_type=jnp.float32)


def product_left(left, right):
    return lax.dot_general(
        left, right, (((0,), (0,)), ((), ())), preferred_element_type=jnp.float32
    )


def product_right(left, right):
    return lax.dot_general(
        left, right, (((1,), (1,)), ((), ())), preferred_element_type=jnp.float32
    )


def gelu_exact(values):
    return jax.nn.gelu(values, approximate=False)


def normalize(values, gains, shift):
    center = values - jnp.mean(values, axis=-1, keepdims=True)
    inverse = lax.rsqrt(jnp.mean(center * center, axis=-1, keepdims=True) + EPSILON)
    scaled = center * inverse
    return (scaled * gains + shift, scaled, inverse)


def norm_back(grad_normed, scaled, inverse, gains):
    grad_scaled = grad_normed * gains
    return inverse * (
        grad_scaled
        - jnp.mean(grad_scaled, axis=-1, keepdims=True)
        - scaled * jnp.mean(grad_scaled * scaled, axis=-1, keepdims=True)
    )


def key_flags(counts_now, length, capacity):
    position = jnp.arange(length, dtype=jnp.int32)
    owner_index = position // capacity
    devices = jnp.arange(counts_now.shape[0], dtype=jnp.int32)
    owner_count = jnp.sum(
        jnp.where(owner_index[:, None] == devices[None, :], counts_now[None, :], 0), axis=1
    )
    return position % capacity < owner_count


def sweep_blocks(step, carried, arrays, capacity):
    length = arrays[0].shape[0]
    block_size = math.gcd(length, 2 * capacity)
    stacked = tuple(
        (member.reshape((length // block_size, block_size) + member.shape[1:]) for member in arrays)
    )

    def advance(current, pieces):
        return (step(current, *pieces), None)

    result, unused = lax.scan(advance, carried, stacked)
    return result


def block_scores(queries, key_rows, key_live):
    scores = jnp.einsum(
        "qhd,khd->hqk", queries, key_rows, preferred_element_type=jnp.float32
    ) * HD ** (-0.5)
    return jnp.where(key_live[None, None, :], scores, NEGATIVE_FILL)


def stats_step(queries, carried, key_rows, key_live):
    running_top, running_total = carried
    scores = block_scores(queries, key_rows, key_live)
    new_top = jnp.maximum(running_top, jnp.max(scores, axis=-1))
    new_total = running_total * jnp.exp(running_top - new_top) + jnp.sum(
        jnp.exp(scores - new_top[:, :, None]), axis=-1
    )
    return (new_top, new_total)


def value_step(queries, log_total, carried, key_rows, value_rows, key_live):
    high_part, low_part = carried
    weights = jnp.exp(block_scores(queries, key_rows, key_live) - log_total[:, :, None])
    weights_low = weights.astype(jnp.bfloat16)
    remainder = (weights - weights_low.astype(jnp.float32)).astype(jnp.bfloat16)
    high_part = high_part + jnp.einsum(
        "hqk,khd->qhd", weights_low, value_rows, preferred_element_type=jnp.float32
    )
    low_part = low_part + jnp.einsum(
        "hqk,khd->qhd", remainder, value_rows, preferred_element_type=jnp.float32
    )
    return (high_part, low_part)


def query_grad_step(
    queries, log_total, grad_heads, row_delta, carried, key_rows, value_rows, key_live
):
    weights = jnp.exp(block_scores(queries, key_rows, key_live) - log_total[:, :, None])
    grad_weights = jnp.einsum(
        "qhd,khd->hqk", grad_heads, value_rows, preferred_element_type=jnp.float32
    )
    grad_scores = (weights * (grad_weights - row_delta[:, :, None])).astype(jnp.bfloat16)
    return carried + jnp.einsum(
        "hqk,khd->qhd", grad_scores, key_rows, preferred_element_type=jnp.float32
    ) * HD ** (-0.5)


def key_grad_terms(queries, log_total, grad_heads, row_delta, key_rows, value_rows, key_live):
    weights = jnp.exp(block_scores(queries, key_rows, key_live) - log_total[:, :, None])
    grad_weights = jnp.einsum(
        "qhd,khd->hqk", grad_heads, value_rows, preferred_element_type=jnp.float32
    )
    grad_scores = (weights * (grad_weights - row_delta[:, :, None])).astype(jnp.bfloat16)
    grad_keys = jnp.einsum(
        "hqk,qhd->khd", grad_scores, queries, preferred_element_type=jnp.float32
    ) * HD ** (-0.5)
    grad_values = jnp.einsum(
        "hqk,qhd->khd", weights.astype(jnp.bfloat16), grad_heads, preferred_element_type=jnp.float32
    )
    return (grad_keys, grad_values)


def local(
    section_input,
    cotangent,
    counts,
    norm_gain,
    vector_bias,
    qkv_weight,
    head_bias,
    out_weight,
    up_weight,
    up_bias,
    down_weight,
):
    ctx_count = lax.axis_size("ctx")
    ctx_index = lax.axis_index("ctx")
    section_index = lax.axis_index("section")
    micro_count, capacity, width = section_input.shape
    total_rows = capacity * ctx_count
    gathered = (
        lax.all_gather(norm_gain, "ctx", axis=2, tiled=True),
        lax.all_gather(vector_bias, "ctx", axis=2, tiled=True),
        lax.all_gather(qkv_weight, "ctx", axis=2, tiled=True),
        lax.all_gather(head_bias, "ctx", axis=3, tiled=True),
        lax.all_gather(out_weight, "ctx", axis=2, tiled=True),
        lax.all_gather(up_weight, "ctx", axis=1, tiled=True),
        lax.all_gather(up_bias, "ctx", axis=2, tiled=True),
        lax.all_gather(down_weight, "ctx", axis=2, tiled=True),
    )
    gains = gathered[0][0].astype(jnp.float32)
    shifts = gathered[1][0].astype(jnp.float32)
    proj_weight = gathered[2][0]
    head_count = gathered[3].shape[2]
    local_width = head_count * HD
    bias_heads = gathered[3][0].astype(jnp.float32).reshape(2, local_width)
    merge_weight = gathered[4][0]
    expand_weight = gathered[5][0]
    expand_bias = gathered[6][0].astype(jnp.float32).reshape(-1)
    reduce_weight = gathered[7][0]

    def branch_total(partial_rows):
        return lax.psum(partial_rows.astype(jnp.bfloat16), "tp").astype(jnp.float32)

    def grad_sum(partial_rows):
        return lax.psum(partial_rows.astype(jnp.bfloat16), "tp").astype(jnp.float32)

    def as_heads(matrix):
        return matrix.reshape(matrix.shape[0], head_count, HD)

    def attend_backward(queries, held, counts_now, log_total, grad_rows, row_delta):
        query_heads = as_heads(queries)
        grad_heads = as_heads(grad_rows)
        empty_heads = jnp.zeros((capacity, head_count, HD), jnp.float32)
        all_keys, all_values = held
        key_live = key_flags(counts_now, total_rows, capacity)
        grad_query = sweep_blocks(
            partial(query_grad_step, query_heads, log_total, grad_heads, row_delta),
            empty_heads,
            (as_heads(all_keys), as_heads(all_values), key_live),
            capacity,
        )
        length = lax.axis_size("ctx") * capacity
        key_part = as_heads(all_keys)
        value_part = as_heads(all_values)
        live_part = key_flags(counts_now, length, capacity)
        block_size = math.gcd(length, 2 * capacity)
        block_count = length // block_size

        def one_block(pieces):
            grad_keys, grad_values = key_grad_terms(
                query_heads, log_total, grad_heads, row_delta, pieces[0], pieces[1], pieces[2]
            )
            return jnp.concatenate(
                [
                    grad_keys.reshape(block_size, local_width),
                    grad_values.reshape(block_size, local_width),
                ],
                axis=1,
            )

        term_rows = lax.map(
            one_block,
            (
                key_part.reshape(block_count, block_size, head_count, HD),
                value_part.reshape(block_count, block_size, head_count, HD),
                live_part.reshape(block_count, block_size),
            ),
        )
        combined = lax.psum_scatter(
            term_rows.reshape(length, 2 * local_width).astype(jnp.bfloat16),
            "ctx",
            scatter_dimension=0,
            tiled=True,
        ).astype(jnp.float32)
        grad_keys = combined[:, :local_width]
        grad_values = combined[:, local_width:]
        return (grad_query.reshape(capacity, local_width), grad_keys, grad_values)

    def layer_backward(grad_output, kept, counts_now):
        (
            live_rows,
            scaled_one,
            inverse_one,
            normed_low,
            queries,
            held,
            log_total,
            attended,
            exact_out,
            scaled_two,
            inverse_two,
            normed_two_low,
            expanded,
            activated,
        ) = kept
        grad_rows = grad_output * live_rows
        reduce_low = grad_rows.astype(jnp.bfloat16)
        grad_reduce = product_left(activated, reduce_low)
        grad_shift_three = jnp.sum(reduce_low, axis=0, dtype=jnp.float32)
        grad_active = product_right(reduce_low, reduce_weight)
        unused, gelu_back = jax.vjp(gelu_exact, expanded)
        grad_expand = gelu_back(grad_active)[0].astype(jnp.bfloat16)
        grad_expand_weight = product_left(normed_two_low, grad_expand)
        grad_expand_bias = jnp.sum(grad_expand, axis=0, dtype=jnp.float32)
        grad_normed_two = grad_sum(product_right(grad_expand, expand_weight))
        grad_gain_two = jnp.sum(grad_normed_two * scaled_two, axis=0)
        grad_shift_two = jnp.sum(grad_normed_two, axis=0)
        grad_middle = grad_rows + norm_back(grad_normed_two, scaled_two, inverse_two, gains[1])
        middle_low = grad_middle.astype(jnp.bfloat16)
        grad_merge = product_left(attended, middle_low)
        grad_shift_one = jnp.sum(middle_low, axis=0, dtype=jnp.float32)
        grad_attended = product_right(middle_low, merge_weight).astype(jnp.bfloat16)
        row_delta = jnp.sum(
            (grad_attended.astype(jnp.float32) * exact_out).reshape(capacity, head_count, HD),
            axis=2,
        ).T
        grad_query, grad_keys, grad_values = attend_backward(
            queries, held, counts_now, log_total, grad_attended, row_delta
        )
        query_low = grad_query.astype(jnp.bfloat16)
        keys_low = grad_keys.astype(jnp.bfloat16)
        values_low = grad_values.astype(jnp.bfloat16)
        grad_proj = jnp.stack(
            [
                product_left(normed_low, query_low),
                product_left(normed_low, keys_low),
                product_left(normed_low, values_low),
            ]
        )
        grad_heads_bias = jnp.stack(
            [
                jnp.sum(query_low, axis=0, dtype=jnp.float32),
                jnp.sum(values_low, axis=0, dtype=jnp.float32),
            ]
        ).reshape(2, head_count, HD)
        grad_normed = grad_sum(
            product_right(query_low, proj_weight[0])
            + product_right(keys_low, proj_weight[1])
            + product_right(values_low, proj_weight[2])
        )
        grad_gain_one = jnp.sum(grad_normed * scaled_one, axis=0)
        grad_shift_zero = jnp.sum(grad_normed, axis=0)
        grad_entry = grad_middle + norm_back(grad_normed, scaled_one, inverse_one, gains[0])
        grads = (
            jnp.stack([grad_gain_one, grad_gain_two]),
            jnp.stack([grad_shift_zero, grad_shift_one, grad_shift_two, grad_shift_three]),
            grad_proj,
            grad_heads_bias,
            grad_merge,
            grad_expand_weight,
            grad_expand_bias,
            grad_reduce,
        )
        return (grad_entry, grads)

    empty_rows = jnp.zeros((capacity, width), jnp.bfloat16)
    incoming = empty_rows
    produced = []
    memory = []
    for tick_index in range(micro_count + 1):
        own_rows = section_input[tick_index] if tick_index < micro_count else empty_rows
        current = jnp.where(section_index == 0, own_rows, incoming)
        counts_now = jnp.where(
            section_index == 0,
            counts[min(tick_index, micro_count - 1)],
            counts[max(tick_index - 1, 0)],
        )
        residual = current.astype(jnp.float32)
        my_count = jnp.sum(
            jnp.where(jnp.arange(ctx_count, dtype=jnp.int32) == ctx_index, counts_now, 0)
        )
        layer_live_rows = (jnp.arange(capacity, dtype=jnp.int32) < my_count).astype(jnp.float32)[
            :, None
        ]
        normed, layer_scaled_one, layer_inverse_one = normalize(residual, gains[0], shifts[0])
        layer_normed_low = normed.astype(jnp.bfloat16)
        projected = jnp.einsum(
            "rd,cde->cre", layer_normed_low, proj_weight, preferred_element_type=jnp.float32
        )
        layer_queries = (projected[0] + bias_heads[0]).astype(jnp.bfloat16)
        layer_key_rows = projected[1].astype(jnp.bfloat16)
        layer_value_rows = (projected[2] + bias_heads[1]).astype(jnp.bfloat16)
        attend_query_heads = as_heads(layer_queries)
        start_state = (
            jnp.full((head_count, capacity), NEGATIVE_FILL, jnp.float32),
            jnp.zeros((head_count, capacity), jnp.float32),
        )
        attend_empty_heads = jnp.zeros((capacity, head_count, HD), jnp.float32)
        attend_all_keys = lax.all_gather(layer_key_rows, "ctx", axis=0, tiled=True)
        attend_all_values = lax.all_gather(layer_value_rows, "ctx", axis=0, tiled=True)
        attend_key_live = key_flags(counts_now, total_rows, capacity)
        running_top, running_total = sweep_blocks(
            partial(stats_step, attend_query_heads),
            start_state,
            (as_heads(attend_all_keys), attend_key_live),
            capacity,
        )
        attend_log_total = running_top + jnp.log(running_total)
        high_part, low_part = sweep_blocks(
            partial(value_step, attend_query_heads, attend_log_total),
            (attend_empty_heads, attend_empty_heads),
            (as_heads(attend_all_keys), as_heads(attend_all_values), attend_key_live),
            capacity,
        )
        attend_held = (attend_all_keys, attend_all_values)
        layer_attended = high_part.reshape(capacity, local_width).astype(jnp.bfloat16)
        layer_exact_out = (high_part + low_part).reshape(capacity, local_width)
        middle = residual + branch_total(product(layer_attended, merge_weight)) + shifts[1]
        normed_two, layer_scaled_two, layer_inverse_two = normalize(middle, gains[1], shifts[2])
        layer_normed_two_low = normed_two.astype(jnp.bfloat16)
        layer_expanded = product(layer_normed_two_low, expand_weight) + expand_bias
        layer_activated = gelu_exact(layer_expanded).astype(jnp.bfloat16)
        output_rows = (
            middle + branch_total(product(layer_activated, reduce_weight)) + shifts[3]
        ) * layer_live_rows
        layer_kept = (
            layer_live_rows,
            layer_scaled_one,
            layer_inverse_one,
            layer_normed_low,
            layer_queries,
            attend_held,
            attend_log_total,
            layer_attended,
            layer_exact_out,
            layer_scaled_two,
            layer_inverse_two,
            layer_normed_two_low,
            layer_expanded,
            layer_activated,
        )
        output_rows, kept = (output_rows, layer_kept)
        output_low = output_rows.astype(jnp.bfloat16)
        produced.append(output_low)
        memory.append((kept, counts_now))
        if tick_index < micro_count:
            incoming = from_behind(output_low, "section", 1)
    acts = jnp.stack(
        [
            jnp.where(section_index == 0, produced[micro_index], produced[micro_index + 1])
            for micro_index in range(micro_count)
        ]
    )[None]
    returning = empty_rows
    totals = None
    returned = []
    for tick_index in range(micro_count + 1):
        own_rows = (
            cotangent[micro_count - 1 - tick_index] if tick_index < micro_count else empty_rows
        )
        current = jnp.where(section_index == 1, own_rows, returning)
        kept, counts_now = memory[micro_count - tick_index]
        grad_entry, grads = layer_backward(current.astype(jnp.float32), kept, counts_now)
        totals = grads if totals is None else jax.tree.map(jnp.add, totals, grads)
        entry_low = grad_entry.astype(jnp.bfloat16)
        returned.append(entry_low)
        if tick_index < micro_count:
            returning = from_behind(entry_low, "section", -1)
    in_grads = jnp.stack(
        [
            jnp.where(
                section_index == 0,
                returned[micro_count - micro_index],
                returned[micro_count - 1 - micro_index],
            )
            for micro_index in range(micro_count)
        ]
    )[None]
    owned = (
        lax.psum_scatter(
            totals[0][None].astype(jnp.bfloat16), "ctx", scatter_dimension=2, tiled=True
        ).astype(jnp.float32),
        lax.psum_scatter(
            totals[1][None].astype(jnp.bfloat16), "ctx", scatter_dimension=2, tiled=True
        ).astype(jnp.float32),
        lax.psum_scatter(
            totals[2][None].astype(jnp.bfloat16), "ctx", scatter_dimension=2, tiled=True
        ).astype(jnp.float32),
        lax.psum_scatter(
            totals[3][None].astype(jnp.bfloat16), "ctx", scatter_dimension=3, tiled=True
        ).astype(jnp.float32),
        lax.psum_scatter(
            totals[4][None].astype(jnp.bfloat16), "ctx", scatter_dimension=2, tiled=True
        ).astype(jnp.float32),
        lax.psum_scatter(
            totals[5][None].astype(jnp.bfloat16), "ctx", scatter_dimension=1, tiled=True
        ).astype(jnp.float32),
        lax.psum_scatter(
            totals[6].reshape(-1, HD)[None].astype(jnp.bfloat16),
            "ctx",
            scatter_dimension=2,
            tiled=True,
        ).astype(jnp.float32),
        lax.psum_scatter(
            totals[7][None].astype(jnp.bfloat16), "ctx", scatter_dimension=2, tiled=True
        ).astype(jnp.float32),
    )
    return (
        acts,
        in_grads,
        owned[0],
        owned[1],
        owned[2],
        owned[3],
        owned[4],
        owned[5],
        owned[6],
        owned[7],
    )


def solution(mesh):
    in_specs = (
        P(None, "ctx", None),
        P(None, "ctx", None),
        P(),
        P("section", None, "ctx"),
        P("section", None, "ctx"),
        P("section", None, "ctx", "tp"),
        P("section", None, "tp", "ctx"),
        P("section", "tp", "ctx"),
        P("section", "ctx", "tp"),
        P("section", "tp", "ctx"),
        P("section", "tp", "ctx"),
    )
    out_specs = (
        P("section", None, "ctx", None),
        P("section", None, "ctx", None),
        P("section", None, "ctx"),
        P("section", None, "ctx"),
        P("section", None, "ctx", "tp"),
        P("section", None, "tp", "ctx"),
        P("section", "tp", "ctx"),
        P("section", "ctx", "tp"),
        P("section", "tp", "ctx"),
        P("section", "tp", "ctx"),
    )
    return jax.shard_map(local, mesh=mesh, in_specs=in_specs, out_specs=out_specs, check_vma=False)
```

profile of v0, /device:TPU:0, one launch (start us, length us, event | category | flops | bytes accessed | tf_op | source)
XLA Modules:
  0.0 3347.4 jit_solution(842557054077755325)
XLA Ops:
  148.8 46.1 %while.240 = (s32[]{:T(128)}, f32[3,1024]{1,0:T(4,128)}, f32[3,1024]{1,0:T(4,128)}, pred[2,2048]{1,0:T(4,128)(4,1)S(1)}, bf16[2,2048,3,64]{1,3,2,0:T(8,128)(2,1)...) while((s32[]{:T(128)}, f32[3,1024]{1,0:T(4,128)}, f32[3,1024]{1,0:T(4,128)}, ...), condition=%wide.region_6.7_spmd.clone, body=%wide.region_3.6_spmd.clone.sunk | while | flops 849361920 | bytes 51826872 | solution.py:78
  199.7 70.4 %while.241 = (s32[]{:T(128)}, f32[1024,3,64]{0,2,1:T(8,128)}, f32[1024,3,64]{0,2,1:T(8,128)}, bf16[2,2048,3,64]{1,3,2,0:T(8,128)(2,1)}, pred[2,2048]{1,0:T(4,128...) while((s32[]{:T(128)}, f32[1024,3,64]{0,2,1:T(8,128)}, ...), condition=%wide.region_8.9_spmd.clone, body=%wide.region_7.8_spmd.clone.sunk | while | flops 2485911552 | bytes 94016200 | solution.py:78
  386.7 40.6 %all-reduce.23.cloned.1.call-done = bf16[1024,768]{1,0:T(8,128)(2,1)} async-done(((bf16[1024,768]{1,0:T(8,128)(2,1)}), bf16[1024,768]{1,0:T(8,128)(2,1)}) %all-reduce.23.cloned.1.call-update) | async-done | bytes 1572880 | tf_op jit(solution)/shard_map/psum | solution.py:181
  433.8 33.4 collective-permute-done
  474.3 37.3 %all-gather.34.cloned.1.call-done = bf16[1,4096,192]{1,2,0:T(8,128)(2,1)} async-done(((bf16[1,1024,192]{1,2,0:T(8,128)(2,1)}), bf16[1,4096,192]{1,2,0:T(8,128)(2,1)}) %all-gather.34.cloned.1.call-update) | async-done | bytes 1572880 | tf_op jit(solution)/shard_map/all_gather | solution.py:348
  515.0 46.0 %while.242 = (s32[]{:T(128)}, f32[3,1024]{1,0:T(4,128)}, f32[3,1024]{1,0:T(4,128)}, pred[2,2048]{1,0:T(4,128)(4,1)S(1)}, bf16[2,2048,3,64]{1,3,2,0:T(8,128)(2,1)...) while((s32[]{:T(128)}, f32[3,1024]{1,0:T(4,128)}, f32[3,1024]{1,0:T(4,128)}, ...), condition=%wide.region_20.21_spmd.clone, body=%wide.region_17.20_spmd.clone.sunk | while | flops 849361920 | bytes 51826872 | solution.py:78
  566.4 69.8 %while.243 = (s32[]{:T(128)}, f32[1024,3,64]{0,2,1:T(8,128)}, f32[1024,3,64]{0,2,1:T(8,128)}, bf16[2,2048,3,64]{1,3,2,0:T(8,128)(2,1)}, pred[2,2048]{1,0:T(4,128...) while((s32[]{:T(128)}, f32[1024,3,64]{0,2,1:T(8,128)}, ...), condition=%wide.region_22.23_spmd.clone, body=%wide.region_21.22_spmd.clone.sunk | while | flops 2485911552 | bytes 87720088 | solution.py:78
  643.2 42.0 %all-reduce.25.cloned.1.call-done = bf16[1024,768]{1,0:T(8,128)(2,1)} async-done(((bf16[1024,768]{1,0:T(8,128)(2,1)}), bf16[1024,768]{1,0:T(8,128)(2,1)}) %all-reduce.25.cloned.1.call-update) | async-done | bytes 1572880 | tf_op jit(solution)/shard_map/psum | solution.py:181
  703.0 42.3 %all-reduce.27.cloned.1.call-done = bf16[1024,768]{1,0:T(8,128)(2,1)} async-done(((bf16[1024,768]{1,0:T(8,128)(2,1)}), bf16[1024,768]{1,0:T(8,128)(2,1)}) %all-reduce.27.cloned.1.call-update) | async-done | bytes 1572880 | tf_op jit(solution)/shard_map/psum | solution.py:181
  752.5 33.4 collective-permute-done.1
  792.9 37.3 %all-gather.36.cloned.1.call-done = bf16[1,4096,192]{1,2,0:T(8,128)(2,1)} async-done(((bf16[1,1024,192]{1,2,0:T(8,128)(2,1)}), bf16[1,4096,192]{1,2,0:T(8,128)(2,1)}) %all-gather.36.cloned.1.call-update) | async-done | bytes 1572880 | tf_op jit(solution)/shard_map/all_gather | solution.py:348
  833.7 46.0 %while.244 = (s32[]{:T(128)}, f32[3,1024]{1,0:T(4,128)}, f32[3,1024]{1,0:T(4,128)}, pred[2,2048]{1,0:T(4,128)(4,1)S(1)}, bf16[2,2048,3,64]{1,3,2,0:T(8,128)(2,1)...) while((s32[]{:T(128)}, f32[3,1024]{1,0:T(4,128)}, f32[3,1024]{1,0:T(4,128)}, ...), condition=%wide.region_34.35_spmd.clone, body=%wide.region_31.34_spmd.clone.sunk | while | flops 849361920 | bytes 51826872 | solution.py:78
  885.0 70.1 %while.245 = (s32[]{:T(128)}, f32[1024,3,64]{0,2,1:T(8,128)}, f32[1024,3,64]{0,2,1:T(8,128)}, bf16[2,2048,3,64]{1,3,2,0:T(8,128)(2,1)}, pred[2,2048]{1,0:T(4,128...) while((s32[]{:T(128)}, f32[1024,3,64]{0,2,1:T(8,128)}, ...), condition=%wide.region_36.37_spmd.clone, body=%wide.region_35.36_spmd.clone.sunk | while | flops 2485911552 | bytes 87720088 | solution.py:78
  962.2 42.0 %all-reduce.29.cloned.1.call-done = bf16[1024,768]{1,0:T(8,128)(2,1)} async-done(((bf16[1024,768]{1,0:T(8,128)(2,1)}), bf16[1024,768]{1,0:T(8,128)(2,1)}) %all-reduce.29.cloned.1.call-update) | async-done | bytes 1572880 | tf_op jit(solution)/shard_map/psum | solution.py:181
  1021.9 42.3 %all-reduce.31.cloned.1.call-done = bf16[1024,768]{1,0:T(8,128)(2,1)} async-done(((bf16[1024,768]{1,0:T(8,128)(2,1)}), bf16[1024,768]{1,0:T(8,128)(2,1)}) %all-reduce.31.cloned.1.call-update) | async-done | bytes 1572880 | tf_op jit(solution)/shard_map/psum | solution.py:181
  1111.9 37.3 %all-gather.38.cloned.1.call-done = bf16[1,4096,192]{1,2,0:T(8,128)(2,1)} async-done(((bf16[1,1024,192]{1,2,0:T(8,128)(2,1)}), bf16[1,4096,192]{1,2,0:T(8,128)(2,1)}) %all-gather.38.cloned.1.call-update) | async-done | bytes 1572880 | tf_op jit(solution)/shard_map/all_gather | solution.py:348
  1152.7 46.0 %while.246 = (s32[]{:T(128)}, f32[3,1024]{1,0:T(4,128)}, f32[3,1024]{1,0:T(4,128)}, pred[2,2048]{1,0:T(4,128)(4,1)S(1)}, bf16[2,2048,3,64]{1,3,2,0:T(8,128)(2,1)...) while((s32[]{:T(128)}, f32[3,1024]{1,0:T(4,128)}, f32[3,1024]{1,0:T(4,128)}, ...), condition=%wide.region_48.49_spmd.clone, body=%wide.region_45.48_spmd.clone.sunk | while | flops 849361920 | bytes 51826872 | solution.py:78
  1204.0 70.0 %while.247 = (s32[]{:T(128)}, f32[1024,3,64]{0,2,1:T(8,128)}, f32[1024,3,64]{0,2,1:T(8,128)}, bf16[2,2048,3,64]{1,3,2,0:T(8,128)(2,1)}, pred[2,2048]{1,0:T(4,128...) while((s32[]{:T(128)}, f32[1024,3,64]{0,2,1:T(8,128)}, ...), condition=%wide.region_50.51_spmd.clone, body=%wide.region_49.50_spmd.clone.sunk | while | flops 2485911552 | bytes 87720088 | solution.py:78
  1281.0 42.0 %all-reduce.33.cloned.1.call-done = bf16[1024,768]{1,0:T(8,128)(2,1)} async-done(((bf16[1024,768]{1,0:T(8,128)(2,1)}), bf16[1024,768]{1,0:T(8,128)(2,1)}) %all-reduce.33.cloned.1.call-update) | async-done | bytes 1572880 | tf_op jit(solution)/shard_map/psum | solution.py:181
  1340.6 42.4 %all-reduce.35.cloned.1.call-done = bf16[1024,768]{1,0:T(8,128)(2,1)} async-done(((bf16[1024,768]{1,0:T(8,128)(2,1)}), bf16[1024,768]{1,0:T(8,128)(2,1)}) %all-reduce.35.cloned.1.call-update) | async-done | bytes 1572880 | tf_op jit(solution)/shard_map/psum | solution.py:181
  1429.1 37.3 %all-gather.40.cloned.1.call-done = bf16[1,4096,192]{1,2,0:T(8,128)(2,1)} async-done(((bf16[1,1024,192]{1,2,0:T(8,128)(2,1)}), bf16[1,4096,192]{1,2,0:T(8,128)(2,1)}) %all-gather.40.cloned.1.call-update) | async-done | bytes 1572880 | tf_op jit(solution)/shard_map/all_gather | solution.py:348
  1469.9 46.0 %while.248 = (s32[]{:T(128)}, f32[3,1024]{1,0:T(4,128)}, f32[3,1024]{1,0:T(4,128)}, pred[2,2048]{1,0:T(4,128)(4,1)S(1)}, bf16[2,2048,3,64]{1,3,2,0:T(8,128)(2,1)...) while((s32[]{:T(128)}, f32[3,1024]{1,0:T(4,128)}, f32[3,1024]{1,0:T(4,128)}, ...), condition=%wide.region_62.63_spmd.clone, body=%wide.region_59.62_spmd.clone.sunk | while | flops 849361920 | bytes 51826872 | solution.py:78
  1521.2 69.8 %while.249 = (s32[]{:T(128)}, f32[1024,3,64]{0,2,1:T(8,128)}, f32[1024,3,64]{0,2,1:T(8,128)}, bf16[2,2048,3,64]{1,3,2,0:T(8,128)(2,1)}, pred[2,2048]{1,0:T(4,128...) while((s32[]{:T(128)}, f32[1024,3,64]{0,2,1:T(8,128)}, ...), condition=%wide.region_64.65_spmd.clone, body=%wide.region_63.64_spmd.clone.sunk | while | flops 2485911552 | bytes 87720088 | solution.py:78
  1598.6 40.8 %all-reduce.37.cloned.1.call-done = bf16[1024,768]{1,0:T(8,128)(2,1)} async-done(((bf16[1024,768]{1,0:T(8,128)(2,1)}), bf16[1024,768]{1,0:T(8,128)(2,1)}) %all-reduce.37.cloned.1.call-update) | async-done | bytes 1572880 | tf_op jit(solution)/shard_map/psum | solution.py:181
  1661.2 43.0 %all-reduce.39.cloned.1.call-done = bf16[1024,768]{1,0:T(8,128)(2,1)} async-done(((bf16[1024,768]{1,0:T(8,128)(2,1)}), bf16[1024,768]{1,0:T(8,128)(2,1)}) %all-reduce.39.cloned.1.call-update) | async-done | bytes 1572880 | tf_op jit(solution)/shard_map/psum | solution.py:184
  1718.0 83.9 %while.235 = (s32[]{:T(128)}, bf16[2,2048,384]{2,1,0:T(8,128)(2,1)}, pred[2,2048]{1,0:T(4,128)(4,1)S(1)}, bf16[2,2048,3,64]{1,3,2,0:T(8,128)(2,1)S(1)}, bf16[102...) while((s32[]{:T(128)}, bf16[2,2048,384]{2,1,0:T(8,128)(2,1)}, ...), condition=%wide.region_77.78_spmd, body=%wide.region_76.77_spmd.sunk | while | flops 3288072192 | bytes 95999168 | solution.py:220
  1802.6 52.3 %while.250 = (s32[]{:T(128)}, f32[1024,3,64]{0,2,1:T(8,128)}, bf16[2,2048,3,64]{1,3,2,0:T(8,128)(2,1)S(1)}, pred[2,2048]{1,0:T(4,128)(4,1)S(1)}, bf16[1024,3,64]...) while((s32[]{:T(128)}, f32[1024,3,64]{0,2,1:T(8,128)}, ...), condition=%wide.region_75.76_spmd.clone, body=%wide.region_74.75_spmd.clone.sunk | while | flops 2454257664 | bytes 56663192 | solution.py:78
  1866.5 43.0 %all-reduce.41.cloned.1.call-done = bf16[1024,768]{1,0:T(8,128)(2,1)} async-done(((bf16[1024,768]{1,0:T(8,128)(2,1)}), bf16[1024,768]{1,0:T(8,128)(2,1)}) %all-reduce.41.cloned.1.call-update) | async-done | bytes 1572880 | tf_op jit(solution)/shard_map/psum | solution.py:184
  1919.1 36.2 %collective-permute-done.4 = bf16[1024,768]{1,0:T(8,128)(2,1)S(1)} collective-permute-done((bf16[1024,768]{1,0:T(8,128)(2,1)S(1)}, bf16[1024,768]{1,0:T(8,128)(2,1)S(1)}, u32[]{:S(2)}, u32[]{:S(2)}) %collective-permute-start.4) | collective-permute-done | bytes 1572896 | tf_op jit(solution)/shard_map/ppermute | solution.py:19
  1965.7 42.4 %all-reduce.43.cloned.1.call-done = bf16[1024,768]{1,0:T(8,128)(2,1)} async-done(((bf16[1024,768]{1,0:T(8,128)(2,1)}), bf16[1024,768]{1,0:T(8,128)(2,1)}) %all-reduce.43.cloned.1.call-update) | async-done | bytes 1572880 | tf_op jit(solution)/shard_map/psum | solution.py:184
  2021.4 84.0 %while.236 = (s32[]{:T(128)}, bf16[2,2048,384]{2,1,0:T(8,128)(2,1)}, pred[2,2048]{1,0:T(4,128)(4,1)S(1)}, bf16[2,2048,3,64]{1,3,2,0:T(8,128)(2,1)S(1)}, bf16[102...) while((s32[]{:T(128)}, bf16[2,2048,384]{2,1,0:T(8,128)(2,1)}, ...), condition=%wide.region_89.90_spmd, body=%wide.region_88.89_spmd.sunk | while | flops 3288072192 | bytes 95999168 | solution.py:220
  2106.2 52.3 %while.251 = (s32[]{:T(128)}, f32[1024,3,64]{0,2,1:T(8,128)}, bf16[2,2048,3,64]{1,3,2,0:T(8,128)(2,1)S(1)}, pred[2,2048]{1,0:T(4,128)(4,1)S(1)}, bf16[1024,3,64]...) while((s32[]{:T(128)}, f32[1024,3,64]{0,2,1:T(8,128)}, ...), condition=%wide.region_87.88_spmd.clone, body=%wide.region_86.87_spmd.clone.sunk | while | flops 2454257664 | bytes 56663192 | solution.py:78
  2170.1 43.0 %all-reduce.45.cloned.1.call-done = bf16[1024,768]{1,0:T(8,128)(2,1)} async-done(((bf16[1024,768]{1,0:T(8,128)(2,1)}), bf16[1024,768]{1,0:T(8,128)(2,1)}) %all-reduce.45.cloned.1.call-update) | async-done | bytes 1572880 | tf_op jit(solution)/shard_map/psum | solution.py:184
  2222.6 36.3 %collective-permute-done.5 = bf16[1024,768]{1,0:T(8,128)(2,1)S(1)} collective-permute-done((bf16[1024,768]{1,0:T(8,128)(2,1)S(1)}, bf16[1024,768]{1,0:T(8,128)(2,1)S(1)}, u32[]{:S(2)}, u32[]{:S(2)}) %collective-permute-start.5) | collective-permute-done | bytes 1572896 | tf_op jit(solution)/shard_map/ppermute | solution.py:19
  2269.4 42.4 %all-reduce.47.cloned.1.call-done = bf16[1024,768]{1,0:T(8,128)(2,1)} async-done(((bf16[1024,768]{1,0:T(8,128)(2,1)}), bf16[1024,768]{1,0:T(8,128)(2,1)}) %all-reduce.47.cloned.1.call-update) | async-done | bytes 1572880 | tf_op jit(solution)/shard_map/psum | solution.py:184
  2325.0 84.4 %while.237 = (s32[]{:T(128)}, bf16[2,2048,384]{2,1,0:T(8,128)(2,1)}, pred[2,2048]{1,0:T(4,128)(4,1)S(1)}, bf16[2,2048,3,64]{1,3,2,0:T(8,128)(2,1)S(1)}, bf16[102...) while((s32[]{:T(128)}, bf16[2,2048,384]{2,1,0:T(8,128)(2,1)}, ...), condition=%wide.region_101.102_spmd, body=%wide.region_100.101_spmd.sunk | while | flops 3288072192 | bytes 95999168 | solution.py:220
  2410.1 52.4 %while.252 = (s32[]{:T(128)}, f32[1024,3,64]{0,2,1:T(8,128)}, bf16[2,2048,3,64]{1,3,2,0:T(8,128)(2,1)S(1)}, pred[2,2048]{1,0:T(4,128)(4,1)S(1)}, bf16[1024,3,64]...) while((s32[]{:T(128)}, f32[1024,3,64]{0,2,1:T(8,128)}, ...), condition=%wide.region_99.100_spmd.clone, body=%wide.region_98.99_spmd.clone.sunk | while | flops 2454257664 | bytes 56663192 | solution.py:78
  2474.0 43.0 %all-reduce.49.cloned.1.call-done = bf16[1024,768]{1,0:T(8,128)(2,1)} async-done(((bf16[1024,768]{1,0:T(8,128)(2,1)}), bf16[1024,768]{1,0:T(8,128)(2,1)}) %all-reduce.49.cloned.1.call-update) | async-done | bytes 1572880 | tf_op jit(solution)/shard_map/psum | solution.py:184
  2526.5 36.3 %collective-permute-done.6 = bf16[1024,768]{1,0:T(8,128)(2,1)S(1)} collective-permute-done((bf16[1024,768]{1,0:T(8,128)(2,1)S(1)}, bf16[1024,768]{1,0:T(8,128)(2,1)S(1)}, u32[]{:S(2)}, u32[]{:S(2)}) %collective-permute-start.6) | collective-permute-done | bytes 1572896 | tf_op jit(solution)/shard_map/ppermute | solution.py:19
  2573.4 42.4 %all-reduce.51.cloned.1.call-done = bf16[1024,768]{1,0:T(8,128)(2,1)} async-done(((bf16[1024,768]{1,0:T(8,128)(2,1)}), bf16[1024,768]{1,0:T(8,128)(2,1)}) %all-reduce.51.cloned.1.call-update) | async-done | bytes 1572880 | tf_op jit(solution)/shard_map/psum | solution.py:184
  2629.1 84.1 %while.238 = (s32[]{:T(128)}, bf16[2,2048,384]{2,1,0:T(8,128)(2,1)}, pred[2,2048]{1,0:T(4,128)(4,1)S(1)}, bf16[2,2048,3,64]{1,3,2,0:T(8,128)(2,1)S(1)}, bf16[102...) while((s32[]{:T(128)}, bf16[2,2048,384]{2,1,0:T(8,128)(2,1)}, ...), condition=%wide.region_113.114_spmd, body=%wide.region_112.113_spmd.sunk | while | flops 3288072192 | bytes 95999168 | solution.py:220
  2714.0 52.4 %while.253 = (s32[]{:T(128)}, f32[1024,3,64]{0,2,1:T(8,128)}, bf16[2,2048,3,64]{1,3,2,0:T(8,128)(2,1)S(1)}, pred[2,2048]{1,0:T(4,128)(4,1)S(1)}, bf16[1024,3,64]...) while((s32[]{:T(128)}, f32[1024,3,64]{0,2,1:T(8,128)}, ...), condition=%wide.region_111.112_spmd.clone, body=%wide.region_110.111_spmd.clone.sunk | while | flops 2454257664 | bytes 56663192 | solution.py:78
  2777.8 43.0 %all-reduce.53.cloned.1.call-done = bf16[1024,768]{1,0:T(8,128)(2,1)} async-done(((bf16[1024,768]{1,0:T(8,128)(2,1)}), bf16[1024,768]{1,0:T(8,128)(2,1)}) %all-reduce.53.cloned.1.call-update) | async-done | bytes 1572880 | tf_op jit(solution)/shard_map/psum | solution.py:184
  2830.8 36.6 %collective-permute-done.7 = bf16[1024,768]{1,0:T(8,128)(2,1)S(1)} collective-permute-done((bf16[1024,768]{1,0:T(8,128)(2,1)S(1)}, bf16[1024,768]{1,0:T(8,128)(2,1)S(1)}, u32[]{:S(2)}, u32[]{:S(2)}) %collective-permute-start.7) | collective-permute-done | bytes 1572896 | tf_op jit(solution)/shard_map/ppermute | solution.py:19
  2874.9 42.4 %all-reduce.55.cloned.1.call-done = bf16[1024,768]{1,0:T(8,128)(2,1)} async-done(((bf16[1024,768]{1,0:T(8,128)(2,1)}), bf16[1024,768]{1,0:T(8,128)(2,1)}) %all-reduce.55.cloned.1.call-update) | async-done | bytes 1572880 | tf_op jit(solution)/shard_map/psum | solution.py:184
  2930.4 84.1 %while.239 = (s32[]{:T(128)}, bf16[2,2048,384]{2,1,0:T(8,128)(2,1)}, pred[2,2048]{1,0:T(4,128)(4,1)S(1)}, bf16[2,2048,3,64]{1,3,2,0:T(8,128)(2,1)S(1)}, bf16[102...) while((s32[]{:T(128)}, bf16[2,2048,384]{2,1,0:T(8,128)(2,1)}, ...), condition=%wide.region_125.126_spmd, body=%wide.region_124.125_spmd.sunk | while | flops 3288072192 | bytes 96138536 | solution.py:220
  3121.2 52.1 %while.254 = (s32[]{:T(128)}, f32[1024,3,64]{0,2,1:T(8,128)}, bf16[2,2048,3,64]{1,3,2,0:T(8,128)(2,1)S(1)}, pred[2,2048]{1,0:T(4,128)(4,1)S(1)}, bf16[1024,3,64]...) while((s32[]{:T(128)}, f32[1024,3,64]{0,2,1:T(8,128)}, ...), condition=%wide.region_123.124_spmd.clone, body=%wide.region_122.123_spmd.clone.sunk | while | flops 2454257664 | bytes 55090300 | solution.py:78
  3206.8 43.8 %all-reduce.57.cloned.1.call-done = (bf16[1024,768]{1,0:T(8,128)(2,1)}, bf16[1024,768]{1,0:T(8,128)(2,1)}) async-done(((bf16[1024,768]{1,0:T(8,128)(2,1)}, bf16[1024,768]{1,0:T(8,128)(2,1)}), (bf16[1024,768]{1,0:T(8,128)(2,1)}, bf16[1024,768]{1,0:T(8,128)(2,1)})) %all-reduce.57.cloned.1.call-update) | async-done | bytes 3145744 | tf_op jit(solution)/shard_map/psum | solution.py:181
  (1779 shorter events, 2200.0 us)
Async XLA Ops:
  7.2 138.1 %all-gather.32.cloned.1.call-start = ((), (), s32[]{:S(2)}) async-start(), calls=%async_computation.44 | async-start | bytes 1966080 | tf_op jit(solution)/shard_map/all_gather | solution.py:348
  94.9 100.1 %all-gather.18.cloned.1.call-start = ((), (), s32[]{:S(2)}) async-start(), calls=%async_computation.13 | async-start | bytes 1966080 | tf_op jit(solution)/shard_map/all_gather | solution.py:349
  109.3 208.5 %all-reduce.21.cloned.1.call-start = ((), (), s32[]{:S(2)}) async-start(), calls=%async_computation.14 | async-start | bytes 3145728 | tf_op jit(solution)/shard_map/psum | solution.py:181
  275.4 74.4 %all-gather.20.cloned.1.call-start = ((), (), s32[]{:S(2)}) async-start(), calls=%async_computation.15 | async-start | bytes 1474560 | tf_op jit(solution)/shard_map/all_gather | solution.py:165
  276.0 104.8 %all-gather.22.cloned.1.call-start = ((), (), s32[]{:S(2)}) async-start(), calls=%async_computation.16 | async-start | bytes 1474560 | tf_op jit(solution)/shard_map/all_gather | solution.py:167
  276.6 150.7 %all-reduce.23.cloned.1.call-start = ((), (), s32[]{:S(2)}) async-start(), calls=%async_computation.17 | async-start | bytes 3145728 | tf_op jit(solution)/shard_map/psum | solution.py:181
  385.2 126.3 %all-gather.34.cloned.1.call-start = ((), (), s32[]{:S(2)}) async-start(), calls=%async_computation.45 | async-start | bytes 1966080 | tf_op jit(solution)/shard_map/all_gather | solution.py:348
  472.9 88.1 %all-gather.24.cloned.1.call-start = ((), (), s32[]{:S(2)}) async-start(), calls=%async_computation.18 | async-start | bytes 1966080 | tf_op jit(solution)/shard_map/all_gather | solution.py:349
  474.2 211.0 %all-reduce.25.cloned.1.call-start = ((), (), s32[]{:S(2)}) async-start(), calls=%async_computation.19 | async-start | bytes 3145728 | tf_op jit(solution)/shard_map/psum | solution.py:181
  643.2 102.1 %all-reduce.27.cloned.1.call-start = ((), (), s32[]{:S(2)}) async-start(), calls=%async_computation.20 | async-start | bytes 3145728 | tf_op jit(solution)/shard_map/psum | solution.py:181
  702.2 128.0 %all-gather.36.cloned.1.call-start = ((), (), s32[]{:S(2)}) async-start(), calls=%async_computation.46 | async-start | bytes 1966080 | tf_op jit(solution)/shard_map/all_gather | solution.py:348
  791.6 88.1 %all-gather.26.cloned.1.call-start = ((), (), s32[]{:S(2)}) async-start(), calls=%async_computation.21 | async-start | bytes 1966080 | tf_op jit(solution)/shard_map/all_gather | solution.py:349
  792.9 211.4 %all-reduce.29.cloned.1.call-start = ((), (), s32[]{:S(2)}) async-start(), calls=%async_computation.22 | async-start | bytes 3145728 | tf_op jit(solution)/shard_map/psum | solution.py:181
  962.2 102.1 %all-reduce.31.cloned.1.call-start = ((), (), s32[]{:S(2)}) async-start(), calls=%async_computation.23 | async-start | bytes 3145728 | tf_op jit(solution)/shard_map/psum | solution.py:181
  1021.2 128.0 %all-gather.38.cloned.1.call-start = ((), (), s32[]{:S(2)}) async-start(), calls=%async_computation.47 | async-start | bytes 1966080 | tf_op jit(solution)/shard_map/all_gather | solution.py:348
  1110.6 88.1 %all-gather.28.cloned.1.call-start = ((), (), s32[]{:S(2)}) async-start(), calls=%async_computation.24 | async-start | bytes 1966080 | tf_op jit(solution)/shard_map/all_gather | solution.py:349
  1111.8 211.2 %all-reduce.33.cloned.1.call-start = ((), (), s32[]{:S(2)}) async-start(), calls=%async_computation.25 | async-start | bytes 3145728 | tf_op jit(solution)/shard_map/psum | solution.py:181
  1281.0 102.0 %all-reduce.35.cloned.1.call-start = ((), (), s32[]{:S(2)}) async-start(), calls=%async_computation.26 | async-start | bytes 3145728 | tf_op jit(solution)/shard_map/psum | solution.py:181
  1340.0 126.4 %all-gather.40.cloned.1.call-start = ((), (), s32[]{:S(2)}) async-start(), calls=%async_computation.48 | async-start | bytes 1966080 | tf_op jit(solution)/shard_map/all_gather | solution.py:348
  1427.8 88.1 %all-gather.30.cloned.1.call-start = ((), (), s32[]{:S(2)}) async-start(), calls=%async_computation.27 | async-start | bytes 1966080 | tf_op jit(solution)/shard_map/all_gather | solution.py:349
  1429.0 210.4 %all-reduce.37.cloned.1.call-start = ((), (), s32[]{:S(2)}) async-start(), calls=%async_computation.28 | async-start | bytes 3145728 | tf_op jit(solution)/shard_map/psum | solution.py:181
  1597.3 107.0 %all-reduce.39.cloned.1.call-start = ((), (), s32[]{:S(2)}) async-start(), calls=%async_computation.29 | async-start | bytes 3145728 | tf_op jit(solution)/shard_map/psum | solution.py:184
  1661.2 201.2 %reduce-scatter.28.cloned.1.call-start = ((), (), s32[]{:S(2)}) async-start(), calls=%async_computation.30 | async-start | bytes 3932160 | tf_op jit(solution)/shard_map/reduce_scatter | solution.py:228
  1801.9 107.6 %all-reduce.41.cloned.1.call-start = ((), (), s32[]{:S(2)}) async-start(), calls=%async_computation.31 | async-start | bytes 3145728 | tf_op jit(solution)/shard_map/psum | solution.py:184
  1866.4 141.7 %all-reduce.43.cloned.1.call-start = ((), (), s32[]{:S(2)}) async-start(), calls=%async_computation.32 | async-start | bytes 3145728 | tf_op jit(solution)/shard_map/psum | solution.py:184
  1917.1 38.1 %collective-permute-start.4 = (bf16[1024,768]{1,0:T(8,128)(2,1)S(1)}, bf16[1024,768]{1,0:T(8,128)(2,1)S(1)}, u32[]{:S(2)}, u32[]{:S(2)}) collective-permute-start(bf16[1024,768]{1,0:T(8,128)(2,1)S(1)} %fusion.462), channel_id=1, source_target_pairs={{16,0},{17,1},{18,2},{19,3},{20,4},{21,5},{22,6},{23,7},{24,8},{25... | collective-permute-start | bytes 4718600 | tf_op jit(solution)/shard_map/ppermute | solution.py:19
  1965.7 200.3 %reduce-scatter.30.cloned.1.call-start = ((), (), s32[]{:S(2)}) async-start(), calls=%async_computation.33 | async-start | bytes 3932160 | tf_op jit(solution)/shard_map/reduce_scatter | solution.py:228
  2105.4 107.6 %all-reduce.45.cloned.1.call-start = ((), (), s32[]{:S(2)}) async-start(), calls=%async_computation.34 | async-start | bytes 3145728 | tf_op jit(solution)/shard_map/psum | solution.py:184
  2170.0 141.7 %all-reduce.47.cloned.1.call-start = ((), (), s32[]{:S(2)}) async-start(), calls=%async_computation.35 | async-start | bytes 3145728 | tf_op jit(solution)/shard_map/psum | solution.py:184
  2220.6 38.3 %collective-permute-start.5 = (bf16[1024,768]{1,0:T(8,128)(2,1)S(1)}, bf16[1024,768]{1,0:T(8,128)(2,1)S(1)}, u32[]{:S(2)}, u32[]{:S(2)}) collective-permute-start(bf16[1024,768]{1,0:T(8,128)(2,1)S(1)} %get-tuple-element.2709), channel_id=1, source_target_pairs={{16,0},{17,1},{18,2},{19,3},{20,4},{21,5},{22,6},{23,7},{24,8},{25... | collective-permute-start | bytes 4718600 | tf_op jit(solution)/shard_map/ppermute | solution.py:19
  2269.3 200.6 %reduce-scatter.32.cloned.1.call-start = ((), (), s32[]{:S(2)}) async-start(), calls=%async_computation.36 | async-start | bytes 3932160 | tf_op jit(solution)/shard_map/reduce_scatter | solution.py:228
  2409.4 107.6 %all-reduce.49.cloned.1.call-start = ((), (), s32[]{:S(2)}) async-start(), calls=%async_computation.37 | async-start | bytes 3145728 | tf_op jit(solution)/shard_map/psum | solution.py:184
  2474.0 141.8 %all-reduce.51.cloned.1.call-start = ((), (), s32[]{:S(2)}) async-start(), calls=%async_computation.38 | async-start | bytes 3145728 | tf_op jit(solution)/shard_map/psum | solution.py:184
  2524.6 38.3 %collective-permute-start.6 = (bf16[1024,768]{1,0:T(8,128)(2,1)S(1)}, bf16[1024,768]{1,0:T(8,128)(2,1)S(1)}, u32[]{:S(2)}, u32[]{:S(2)}) collective-permute-start(bf16[1024,768]{1,0:T(8,128)(2,1)S(1)} %get-tuple-element.2707), channel_id=1, source_target_pairs={{16,0},{17,1},{18,2},{19,3},{20,4},{21,5},{22,6},{23,7},{24,8},{25... | collective-permute-start | bytes 4718600 | tf_op jit(solution)/shard_map/ppermute | solution.py:19
  2573.4 200.4 %reduce-scatter.34.cloned.1.call-start = ((), (), s32[]{:S(2)}) async-start(), calls=%async_computation.39 | async-start | bytes 3932160 | tf_op jit(solution)/shard_map/reduce_scatter | solution.py:228
  2713.2 107.6 %all-reduce.53.cloned.1.call-start = ((), (), s32[]{:S(2)}) async-start(), calls=%async_computation.40 | async-start | bytes 3145728 | tf_op jit(solution)/shard_map/psum | solution.py:184
  2777.8 139.5 %all-reduce.55.cloned.1.call-start = ((), (), s32[]{:S(2)}) async-start(), calls=%async_computation.41 | async-start | bytes 3145728 | tf_op jit(solution)/shard_map/psum | solution.py:184
  2829.6 37.9 %collective-permute-start.7 = (bf16[1024,768]{1,0:T(8,128)(2,1)S(1)}, bf16[1024,768]{1,0:T(8,128)(2,1)S(1)}, u32[]{:S(2)}, u32[]{:S(2)}) collective-permute-start(bf16[1024,768]{1,0:T(8,128)(2,1)S(1)} %get-tuple-element.2705), channel_id=1, source_target_pairs={{16,0},{17,1},{18,2},{19,3},{20,4},{21,5},{22,6},{23,7},{24,8},{25... | collective-permute-start | bytes 4718600 | tf_op jit(solution)/shard_map/ppermute | solution.py:19
  2874.9 302.7 %reduce-scatter.36.cloned.1.call-start = ((), (), s32[]{:S(2)}) async-start(), calls=%async_computation.42 | async-start | bytes 3932160 | tf_op jit(solution)/shard_map/reduce_scatter | solution.py:228
  3014.6 172.6 %reduce-scatter.50.cloned.1.call-start = ((), (), s32[]{:S(2)}) async-start(), calls=%async_computation.54 | async-start | bytes 20480
  3067.4 124.7 %reduce-scatter.48.cloned.1.call-start = ((), (), s32[]{:S(2)}) async-start(), calls=%async_computation.53 | async-start | bytes 491520
  3077.9 116.1 %reduce-scatter.52.cloned.1.call-start = ((), (), s32[]{:S(2)}) async-start(), calls=%async_computation.55 | async-start | bytes 1474560
  3094.5 102.3 %reduce-scatter.38.cloned.1.call-start = ((), (), s32[]{:S(2)}) async-start(), calls=%async_computation.43 | async-start | bytes 1474560 | tf_op jit(solution)/shard_map/reduce_scatter | solution.py:444
  3120.7 130.0 %all-reduce.57.cloned.1.call-start = ((), (), s32[]{:S(2)}) async-start(), calls=%async_computation.56 | async-start | bytes 6291456 | tf_op jit(solution)/shard_map/psum | solution.py:181
  3181.7 90.2 %reduce-scatter.46.cloned.1.call-start = ((), (), s32[]{:S(2)}) async-start(), calls=%async_computation.52 | async-start | bytes 20480
  3199.8 92.0 %reduce-scatter.40.cloned.1.call-start = ((), (), s32[]{:S(2)}) async-start(), calls=%async_computation.49 | async-start | bytes 245760
  3255.1 56.5 %reduce-scatter.42.cloned.1.call-start = ((), (), s32[]{:S(2)}) async-start(), calls=%async_computation.50 | async-start | bytes 245760
  3256.5 81.8 %reduce-scatter.44.cloned.1.call-start = ((), (), s32[]{:S(2)}) async-start(), calls=%async_computation.51 | async-start | bytes 1228800
  (539 other events, 8968.0 us)
Sparse Core Ops, SparseCore 0:
  95.0 50.3 all-gather.31
  147.5 36.3 all-gather.17
  275.5 42.2 all-reduce.20
  319.3 30.5 all-gather.19
  351.2 29.5 all-gather.21
  385.3 41.9 all-reduce.22
  473.1 38.4 all-gather.33
  513.7 35.9 all-gather.23
  643.3 41.9 all-reduce.24
  702.3 42.8 all-reduce.26
  791.7 38.4 all-gather.35
  832.2 35.9 all-gather.25
  962.3 41.9 all-reduce.28
  1021.3 42.8 all-reduce.30
  1110.7 38.4 all-gather.37
  1151.2 35.9 all-gather.27
  1281.1 41.9 all-reduce.32
  1340.1 42.9 all-reduce.34
  1427.9 38.4 all-gather.39
  1468.3 35.9 all-gather.29
  1597.4 41.9 all-reduce.36
  1661.3 42.9 all-reduce.38
  1802.0 60.3 reduce-scatter.27
  1866.6 42.8 all-reduce.40
  1965.8 42.2 all-reduce.42
  2105.6 60.3 reduce-scatter.29
  2170.2 42.8 all-reduce.44
  2269.4 42.2 all-reduce.46
  2409.5 60.2 reduce-scatter.31
  2474.1 42.8 all-reduce.48
  2573.5 42.2 all-reduce.50
  2713.4 60.2 reduce-scatter.33
  2777.9 42.8 all-reduce.52
  2875.0 42.2 all-reduce.54
  3014.7 60.3 reduce-scatter.35
  3077.1 18.8 reduce-scatter.49
  3098.9 18.8 reduce-scatter.47
  3120.1 27.3 reduce-scatter.51
  3149.6 27.9 reduce-scatter.37
  3181.9 68.7 all-reduce.56
  3252.9 18.9 reduce-scatter.45
  3274.2 17.5 reduce-scatter.39
  3293.9 17.5 reduce-scatter.41
  3314.0 24.2 reduce-scatter.43
where the time goes:
time: 3360 us; the launch traced here: 3350 us
  waiting for transfers between devices  1330 us (40%)
  matrix products  1320 us (39%)
  other arithmetic  309 us (9%)
  local copies, waits for them, and re-layouts  225 us (7%)
  blocking collectives  116 us (3%)
    dot_general x40, matrix products, block_scores(): jnp.einsum('qhd,khd->hqk', queries, key_rows, preferred_element_type=jnp....  419 us
    psum x10, waiting for transfers between devices, branch_total(): return lax.psum(partial_rows.astype(jnp.bfloat16), 'tp').astype(jnp.float32)  406 us
    psum x9, waiting for transfers between devices, grad_sum(): return lax.psum(partial_rows.astype(jnp.bfloat16), 'tp').astype(jnp.float32)  384 us
    ppermute x8, waiting for transfers between devices, from_behind(): return lax.ppermute(block, axis, route)  279 us
    dot_general x10, matrix products, key_grad_terms(): jnp.einsum('hqk,qhd->khd', grad_scores, queries, preferred_element_type=j...  158 us
    dot_general x10, matrix products, query_grad_step(): jnp.einsum('hqk,khd->qhd', grad_scores, key_rows, preferred_element_type=...  155 us
    all_gather x5, waiting for transfers between devices, local(): attend_all_keys = lax.all_gather(layer_key_rows, 'ctx', axis=0, tiled=True)  154 us
    dot_general x10, matrix products, value_step(): jnp.einsum('hqk,khd->qhd', remainder, value_rows, preferred_element_type=...  125 us
  transfers between devices with their start and end apart: 52, of which 42 were waited for; matrix products, arithmetic and copies ran while one was open for 21% of the time, Pallas kernels for 0%

commit v1 on v0

v1 whole, which is shorter than its diff:
```python
from functools import partial

import jax
import jax.numpy as jnp
from jax import lax
from jax.experimental import pallas as pl
from jax.experimental.pallas import tpu as pltpu
from jax.sharding import PartitionSpec as P

HD = 64
EPSILON = 1e-06
VMEM_BYTES = 48 * 1024 * 1024


def from_behind(block, axis, distance):
    devices = range(lax.axis_size(axis))
    route = [(i - distance, i) for i in devices if i - distance in devices]
    return lax.ppermute(block, axis, route)


def contract(left, right, left_dim, right_dim):
    return lax.dot_general(
        left,
        right,
        (((left_dim,), (right_dim,)), ((), ())),
        preferred_element_type=jnp.float32,
    )


def product(left, right):
    return contract(left, right, 1, 0)


def product_left(left, right):
    return contract(left, right, 0, 0)


def product_right(left, right):
    return contract(left, right, 1, 1)


def gelu_exact(values):
    return jax.nn.gelu(values, approximate=False)


def normalize(values, gains, shift):
    center = values - jnp.mean(values, axis=-1, keepdims=True)
    inverse = lax.rsqrt(jnp.mean(center * center, axis=-1, keepdims=True) + EPSILON)
    scaled = center * inverse
    return (scaled * gains + shift, scaled, inverse)


def norm_back(grad_normed, scaled, inverse, gains):
    grad_scaled = grad_normed * gains
    return inverse * (
        grad_scaled
        - jnp.mean(grad_scaled, axis=-1, keepdims=True)
        - scaled * jnp.mean(grad_scaled * scaled, axis=-1, keepdims=True)
    )


def attend_kernel(heads, query_ref, held_ref, out_ref, log_ref):
    width = heads * HD
    for head in range(heads):
        keys = held_ref[:, head * HD : (head + 1) * HD]
        values = held_ref[:, width + head * HD : width + (head + 1) * HD]
        queries = query_ref[:, head * HD : (head + 1) * HD]
        scores = product_right(keys, queries) * HD ** (-0.5)
        top = jnp.max(scores, axis=0, keepdims=True)
        weights = jnp.exp(scores - top)
        total = jnp.sum(weights, axis=0, keepdims=True)
        mixed = product_left(values, weights.astype(jnp.bfloat16))
        out_ref[head * HD : (head + 1) * HD, :] = mixed / total
        log_ref[head : head + 1, :] = top + jnp.log(total)


def attend(queries, held, heads):
    rows, width = queries.shape
    length = held.shape[0]
    block = min(rows, 256)
    work = rows * length * width
    return pl.pallas_call(
        partial(attend_kernel, heads),
        grid=(rows // block,),
        in_specs=[
            pl.BlockSpec((block, width), lambda i: (i, 0)),
            pl.BlockSpec((length, 2 * width), lambda i: (0, 0)),
        ],
        out_specs=[
            pl.BlockSpec((width, block), lambda i: (0, i)),
            pl.BlockSpec((heads, block), lambda i: (0, i)),
        ],
        out_shape=[
            jax.ShapeDtypeStruct((width, rows), jnp.float32),
            jax.ShapeDtypeStruct((heads, rows), jnp.float32),
        ],
        compiler_params=pltpu.CompilerParams(vmem_limit_bytes=VMEM_BYTES),
        cost_estimate=pl.CostEstimate(
            flops=4 * work, bytes_accessed=4 * length * width, transcendentals=work // HD
        ),
    )(queries, held)


def attend_back_kernel(
    heads, query_ref, held_ref, grad_ref, log_ref, delta_ref, grad_query_ref, grad_held_ref
):
    width = heads * HD
    block = pl.program_id(0)

    @pl.when(block == 0)
    def _():
        grad_held_ref[...] = jnp.zeros_like(grad_held_ref)

    for head in range(heads):
        low, high = head * HD, (head + 1) * HD
        keys = held_ref[:, low:high]
        values = held_ref[:, width + low : width + high]
        queries = query_ref[:, low:high]
        grads = grad_ref[:, low:high]
        scores = product_right(keys, queries) * HD ** (-0.5)
        weights = jnp.exp(scores - log_ref[head : head + 1, :])
        grad_weights = product_right(values, grads)
        grad_scores = weights * (grad_weights - delta_ref[head : head + 1, :])
        grad_scores = grad_scores.astype(jnp.bfloat16)
        grad_query_ref[low:high, :] = product_left(keys, grad_scores) * HD ** (-0.5)
        grad_held_ref[:, low:high] += product(grad_scores, queries) * HD ** (-0.5)
        grad_held_ref[:, width + low : width + high] += product(
            weights.astype(jnp.bfloat16), grads
        )


def attend_back(queries, held, grad_rows, log_total, row_delta, heads):
    rows, width = queries.shape
    length = held.shape[0]
    block = min(rows, 256)
    work = rows * length * width
    return pl.pallas_call(
        partial(attend_back_kernel, heads),
        grid=(rows // block,),
        in_specs=[
            pl.BlockSpec((block, width), lambda i: (i, 0)),
            pl.BlockSpec((length, 2 * width), lambda i: (0, 0)),
            pl.BlockSpec((block, width), lambda i: (i, 0)),
            pl.BlockSpec((heads, block), lambda i: (0, i)),
            pl.BlockSpec((heads, block), lambda i: (0, i)),
        ],
        out_specs=[
            pl.BlockSpec((width, block), lambda i: (0, i)),
            pl.BlockSpec((length, 2 * width), lambda i: (0, 0)),
        ],
        out_shape=[
            jax.ShapeDtypeStruct((width, rows), jnp.float32),
            jax.ShapeDtypeStruct((length, 2 * width), jnp.float32),
        ],
        compiler_params=pltpu.CompilerParams(vmem_limit_bytes=VMEM_BYTES),
        cost_estimate=pl.CostEstimate(
            flops=10 * work, bytes_accessed=12 * length * width, transcendentals=work // HD
        ),
    )(queries, held, grad_rows, log_total, row_delta)


def local(
    section_input,
    cotangent,
    counts,
    norm_gain,
    vector_bias,
    qkv_weight,
    head_bias,
    out_weight,
    up_weight,
    up_bias,
    down_weight,
):
    ctx_count = lax.axis_size("ctx")
    ctx_index = lax.axis_index("ctx")
    tp_count = lax.axis_size("tp")
    tp_index = lax.axis_index("tp")
    section_index = lax.axis_index("section")
    micro_count, capacity, width = section_input.shape
    share = capacity // 2
    half = share // 2
    head_count = head_bias.shape[2]
    local_width = head_count * HD

    small = (norm_gain, vector_bias, head_bias, up_bias)
    packed = jnp.concatenate([member.reshape(-1) for member in small])
    packed_all = lax.all_gather(packed, "ctx", axis=0, tiled=False)
    opened = []
    start = 0
    for member in small:
        part = packed_all[:, start : start + member.size].reshape((ctx_count,) + member.shape[1:])
        part = jnp.moveaxis(part, 0, -2)
        opened.append(part.reshape(part.shape[:-2] + (part.shape[-2] * part.shape[-1],)))
        start += member.size
    gains = opened[0].astype(jnp.float32)
    shifts = opened[1].astype(jnp.float32)
    bias_heads = opened[2].astype(jnp.float32).reshape(2, local_width)
    expand_bias = opened[3].astype(jnp.float32).reshape(-1)
    proj_weight = lax.all_gather(qkv_weight[0], "ctx", axis=1, tiled=True)
    merge_weight = lax.all_gather(out_weight[0], "ctx", axis=1, tiled=True)
    expand_weight = lax.all_gather(up_weight[0], "ctx", axis=0, tiled=True)
    reduce_weight = lax.all_gather(down_weight[0], "ctx", axis=1, tiled=True)

    surplus = jnp.maximum(counts - share, 0)
    deficit = jnp.maximum(share - counts, 0)
    surplus_start = jnp.cumsum(surplus, axis=1) - surplus
    deficit_start = jnp.cumsum(deficit, axis=1) - deficit
    mine = jnp.arange(ctx_count, dtype=jnp.int32) == ctx_index
    my_count = jnp.sum(jnp.where(mine, counts, 0), axis=1)
    my_surplus = jnp.sum(jnp.where(mine, surplus, 0), axis=1)
    my_start = jnp.sum(jnp.where(mine, surplus_start, 0), axis=1)
    slots = (share - half) + jnp.arange(half, dtype=jnp.int32)
    source = (
        deficit_start[:, :, None]
        + slots[None, None, :]
        - counts[:, :, None]
        - my_start[:, None, None]
    )
    free = slots[None, None, :] >= counts[:, :, None]
    past = jnp.arange(share, dtype=jnp.int32)
    chosen = (
        (source[:, :, :, None] == past)
        & free[:, :, :, None]
        & (past[None, :] < my_surplus[:, None])[:, None, None, :]
    ).astype(jnp.bfloat16)
    own_slot = slots[None, :] < my_count[:, None]
    piece = half // tp_count
    strip = width // tp_count

    def spread(rows, first, last):
        picked = lax.dynamic_slice_in_dim(chosen[first:last], tp_index * piece, piece, 2)
        sent = jnp.einsum(
            "mjrc,mcd->mjrd", picked, rows[first:last, share:], preferred_element_type=jnp.float32
        ).astype(jnp.bfloat16)
        got = lax.psum_scatter(sent, "ctx", scatter_dimension=1, tiled=True)[:, 0]
        got = lax.all_gather(got, "tp", axis=1, tiled=True)
        tail = jnp.where(own_slot[first:last, :, None], rows[first:last, share - half : share], got)
        return jnp.concatenate([rows[first:last, : share - half], tail], axis=1)

    def restore(rows, first, last):
        mine_part = lax.dynamic_slice_in_dim(rows[:, share - half :], tp_index * strip, strip, 2)
        every = lax.all_gather(mine_part, "ctx", axis=1, tiled=False)
        back = jnp.einsum(
            "mjrc,mjrd->mcd", chosen[first:last], every, preferred_element_type=jnp.float32
        ).astype(jnp.bfloat16)
        back = lax.all_gather(back, "tp", axis=2, tiled=True)
        tail = jnp.where(own_slot[first:last, :, None], rows[:, share - half :], 0)
        return jnp.concatenate([rows[:, : share - half], tail, back], axis=1)

    entering = jnp.where(section_index == 0, section_input, cotangent)
    entry_first = spread(entering, 0, 1)
    entry_rest = spread(entering, 1, micro_count)
    entry_rows = [entry_first[0]] + [entry_rest[i] for i in range(micro_count - 1)]

    def tp_total(partial_rows):
        return lax.psum(partial_rows.astype(jnp.bfloat16), "tp").astype(jnp.float32)

    def layer_forward(current):
        residual = current.astype(jnp.float32)
        normed, scaled_one, inverse_one = normalize(residual, gains[0], shifts[0])
        normed_low = normed.astype(jnp.bfloat16)
        held_part = jnp.concatenate(
            [
                product(normed_low, proj_weight[1]),
                product(normed_low, proj_weight[2]) + bias_heads[1],
            ],
            axis=1,
        ).astype(jnp.bfloat16)
        held = lax.all_gather(held_part, "ctx", axis=0, tiled=True)
        queries = (product(normed_low, proj_weight[0]) + bias_heads[0]).astype(jnp.bfloat16)
        exact_out, log_total = attend(queries, held, head_count)
        attended = exact_out.astype(jnp.bfloat16)
        middle = residual + tp_total(product_left(attended, merge_weight)) + shifts[1]
        normed_two, scaled_two, inverse_two = normalize(middle, gains[1], shifts[2])
        normed_two_low = normed_two.astype(jnp.bfloat16)
        expanded = product(normed_two_low, expand_weight) + expand_bias
        activated = gelu_exact(expanded).astype(jnp.bfloat16)
        output_rows = middle + tp_total(product(activated, reduce_weight)) + shifts[3]
        kept = (
            scaled_one,
            inverse_one,
            normed_low,
            queries,
            held,
            log_total,
            exact_out,
            attended,
            scaled_two,
            inverse_two,
            normed_two_low,
            expanded,
            activated,
        )
        return output_rows.astype(jnp.bfloat16), kept

    def layer_backward(grad_low, kept):
        (
            scaled_one,
            inverse_one,
            normed_low,
            queries,
            held,
            log_total,
            exact_out,
            attended,
            scaled_two,
            inverse_two,
            normed_two_low,
            expanded,
            activated,
        ) = kept
        grad_rows = grad_low.astype(jnp.float32)
        grad_active = product_right(grad_low, reduce_weight)
        unused, gelu_back = jax.vjp(gelu_exact, expanded)
        grad_expand = gelu_back(grad_active)[0].astype(jnp.bfloat16)
        grad_normed_two = tp_total(product_right(grad_expand, expand_weight))
        grad_reduce = product_left(activated, grad_low)
        grad_shift_three = jnp.sum(grad_rows, axis=0)
        grad_expand_weight = product_left(normed_two_low, grad_expand)
        grad_expand_bias = jnp.sum(grad_expand, axis=0, dtype=jnp.float32)
        grad_gain_two = jnp.sum(grad_normed_two * scaled_two, axis=0)
        grad_shift_two = jnp.sum(grad_normed_two, axis=0)
        grad_middle = grad_rows + norm_back(grad_normed_two, scaled_two, inverse_two, gains[1])
        middle_low = grad_middle.astype(jnp.bfloat16)
        grad_attended = product_right(middle_low, merge_weight).astype(jnp.bfloat16)
        row_delta = jnp.sum(
            (grad_attended.astype(jnp.float32).T * exact_out).reshape(head_count, HD, share), axis=1
        )
        grad_query, grad_held = attend_back(
            queries, held, grad_attended, log_total, row_delta, head_count
        )
        held_low = lax.psum_scatter(
            grad_held.astype(jnp.bfloat16), "ctx", scatter_dimension=0, tiled=True
        )
        grad_merge = product(attended, middle_low)
        grad_shift_one = jnp.sum(middle_low, axis=0, dtype=jnp.float32)
        query_low = grad_query.astype(jnp.bfloat16)
        keys_low = held_low[:, :local_width]
        values_low = held_low[:, local_width:]
        grad_normed = tp_total(
            contract(query_low, proj_weight[0], 0, 1)
            + product_right(keys_low, proj_weight[1])
            + product_right(values_low, proj_weight[2])
        )
        grad_proj = jnp.stack(
            [
                contract(normed_low, query_low, 0, 1),
                product_left(normed_low, keys_low),
                product_left(normed_low, values_low),
            ]
        )
        grad_heads_bias = jnp.stack(
            [
                jnp.sum(query_low, axis=1, dtype=jnp.float32),
                jnp.sum(values_low, axis=0, dtype=jnp.float32),
            ]
        ).reshape(2, head_count, HD)
        grad_gain_one = jnp.sum(grad_normed * scaled_one, axis=0)
        grad_shift_zero = jnp.sum(grad_normed, axis=0)
        grad_entry = grad_middle + norm_back(grad_normed, scaled_one, inverse_one, gains[0])
        grads = (
            jnp.stack([grad_gain_one, grad_gain_two]),
            jnp.stack([grad_shift_zero, grad_shift_one, grad_shift_two, grad_shift_three]),
            grad_heads_bias,
            grad_expand_bias.reshape(-1, HD),
            grad_proj,
            grad_merge,
            grad_expand_weight,
            grad_reduce,
        )
        return (grad_entry.astype(jnp.bfloat16), grads)

    empty_rows = jnp.zeros((share, width), jnp.bfloat16)
    incoming = empty_rows
    produced = []
    memory = []
    for tick_index in range(micro_count + 1):
        own_rows = entry_rows[tick_index] if tick_index < micro_count else empty_rows
        current = jnp.where(section_index == 0, own_rows, incoming)
        output_low, kept = layer_forward(current)
        produced.append(output_low)
        memory.append(kept)
        if tick_index < micro_count:
            incoming = from_behind(output_low, "section", 1)
    acts = restore(
        jnp.stack(
            [
                jnp.where(section_index == 0, produced[i], produced[i + 1])
                for i in range(micro_count)
            ]
        ),
        0,
        micro_count,
    )[None]
    returning = empty_rows
    totals = None
    returned = []
    for tick_index in range(micro_count + 1):
        own_rows = (
            entry_rows[micro_count - 1 - tick_index] if tick_index < micro_count else empty_rows
        )
        current = jnp.where(section_index == 1, own_rows, returning)
        entry_low, grads = layer_backward(current, memory[micro_count - tick_index])
        totals = grads if totals is None else jax.tree.map(jnp.add, totals, grads)
        returned.append(entry_low)
        if tick_index < micro_count:
            returning = from_behind(entry_low, "section", -1)
    grad_inputs = [
        jnp.where(section_index == 0, returned[micro_count - i], returned[micro_count - 1 - i])
        for i in range(micro_count)
    ]
    in_grads = jnp.concatenate(
        [
            restore(grad_inputs[0][None], 0, 1),
            restore(jnp.stack(grad_inputs[1:]), 1, micro_count),
        ]
    )[None]

    def owned(total, dimension):
        return lax.psum_scatter(
            total.astype(jnp.bfloat16), "ctx", scatter_dimension=dimension, tiled=True
        ).astype(jnp.float32)[None]

    small_totals = []
    for total in totals[:4]:
        split = total.reshape(total.shape[:-1] + (ctx_count, total.shape[-1] // ctx_count))
        small_totals.append(jnp.moveaxis(split, -2, 0).reshape(ctx_count, -1))
    small_owned = lax.psum_scatter(
        jnp.concatenate(small_totals, axis=1).astype(jnp.bfloat16),
        "ctx",
        scatter_dimension=0,
        tiled=True,
    )[0].astype(jnp.float32)
    small_out = []
    start = 0
    for member in small:
        small_out.append(small_owned[start : start + member.size].reshape(member.shape))
        start += member.size
    return (
        acts,
        in_grads,
        small_out[0],
        small_out[1],
        owned(totals[4], 1),
        small_out[2],
        owned(totals[5], 1),
        owned(totals[6], 0),
        small_out[3],
        owned(totals[7], 1),
    )


def solution(mesh):
    in_specs = (
        P(None, "ctx", None),
        P(None, "ctx", None),
        P(),
        P("section", None, "ctx"),
        P("section", None, "ctx"),
        P("section", None, "ctx", "tp"),
        P("section", None, "tp", "ctx"),
        P("section", "tp", "ctx"),
        P("section", "ctx", "tp"),
        P("section", "tp", "ctx"),
        P("section", "tp", "ctx"),
    )
    out_specs = (
        P("section", None, "ctx", None),
        P("section", None, "ctx", None),
        P("section", None, "ctx"),
        P("section", None, "ctx"),
        P("section", None, "ctx", "tp"),
        P("section", None, "tp", "ctx"),
        P("section", "tp", "ctx"),
        P("section", "ctx", "tp"),
        P("section", "tp", "ctx"),
        P("section", "tp", "ctx"),
    )
    return jax.shard_map(local, mesh=mesh, in_specs=in_specs, out_specs=out_specs, check_vma=False)
```

time: 3360 us -> 1960 us (0.58)
  matrix products: 1320 us -> 154 us
  other arithmetic: 309 us -> 149 us
  local copies, waits for them, and re-layouts: 225 us -> 141 us
  Pallas kernels: 0 us -> 82.6 us
  waiting for transfers between devices: 1330 us -> 1260 us
    dot_general x165 -> x95, matrix products: 1310 us -> 154 us  [the longest x90 137 us: contract(): lax.dot_general(left, right, (((left_dim,), (right_dim,)), ((), ())), pre...]
    reduce_scatter x6 -> x9, waiting for transfers between devices: 10.2 us -> 255 us  [the longest x5 175 us: layer_backward(): lax.psum_scatter(grad_held.astype(jnp.bfloat16), 'ctx', scatter_dimension...]
    ppermute x8, waiting for transfers between devices: 279 us -> 123 us  [from_behind(): return lax.ppermute(block, axis, route)]
    psum x19, waiting for transfers between devices: 790 us -> 634 us  [tp_total(): return lax.psum(partial_rows.astype(jnp.bfloat16), 'tp').astype(jnp.float32)]
    reduce_sum x25 -> x15, other arithmetic: 135 us -> 7.06 us  [the longest x4 4.46 us: layer_backward(): grad_shift_three = jnp.sum(grad_rows, axis=0)]
    pallas_call x0 -> x10, Pallas kernels: none -> 82.6 us  [the longest x5 45 us: attend_back(): pl.pallas_call(partial(attend_back_kernel, heads), grid=(rows // block,),...]
    unnamed x51 -> x44, waiting for transfers between devices: 53.4 us -> 1.71 us
    all_gather x12, waiting for transfers between devices: 200 us -> 245 us  [the longest x5 164 us: layer_forward(): held = lax.all_gather(held_part, 'ctx', axis=0, tiled=True)]
  transfers between devices with their start and end apart: 52 -> 50, of which waited for: 42 -> 45; matrix products, arithmetic and copies ran while one was open for 21% -> 10% of each run, Pallas kernels for 0% -> 0%
where the time goes in v1:
time: 1960 us; the launch traced here: 1940 us
  waiting for transfers between devices  1260 us (64%)
  matrix products  154 us (8%)
  other arithmetic  149 us (8%)
  local copies, waits for them, and re-layouts  141 us (7%)
  blocking collectives  117 us (6%)
  Pallas kernels  82.6 us (4%)
  starting transfers between devices  24.1 us (1%)
    psum x19, waiting for transfers between devices, tp_total(): return lax.psum(partial_rows.astype(jnp.bfloat16), 'tp').astype(jnp.float32)  634 us
    reduce_scatter x5, waiting for transfers between devices, layer_backward(): lax.psum_scatter(grad_held.astype(jnp.bfloat16), 'ctx', scatter_dimension...  175 us
    all_gather x5, waiting for transfers between devices, layer_forward(): held = lax.all_gather(held_part, 'ctx', axis=0, tiled=True)  164 us
    dot_general x90, matrix products, contract(): lax.dot_general(left, right, (((left_dim,), (right_dim,)), ((), ())), pre...  137 us
    ppermute x8, waiting for transfers between devices, from_behind(): return lax.ppermute(block, axis, route)  123 us
    unnamed x595, local copies, waits for them, and re-layouts  74.6 us
    reduce_scatter x2, waiting for transfers between devices, owned(): lax.psum_scatter(total.astype(jnp.bfloat16), 'ctx', scatter_dimension=dim...  52.7 us
    pallas_call x5, Pallas kernels, attend_back(): pl.pallas_call(partial(attend_back_kernel, heads), grid=(rows // block,),...  45 us
  transfers between devices with their start and end apart: 50, of which 45 were waited for; matrix products, arithmetic and copies ran while one was open for 10% of the time, Pallas kernels for 0%

profile of v1, /device:TPU:0, one launch (start us, length us, event | category | flops | bytes accessed | tf_op | source)
XLA Modules:
  0.0 1944.5 jit_solution(1041694060695900408)
XLA Ops:
  25.6 20.5 %all-reduce = bf16[5760]{0:T(1024)(128)(2,1)S(1)} all-reduce(bf16[5760]{0:T(1024)(128)(2,1)S(1)} %dynamic-update-slice), channel_id=3, replica_groups=mesh['section'=2,'ctx'=4,'tp'=4] {'ctx'}, use_global_device_ids=true, to_apply=%add | all-reduce | flops 5760 | bytes 23040
  46.9 20.7 %all-gather.2 = bf16[1,3,768,192]{3,2,1,0:T(8,128)(2,1)S(1)} all-gather(bf16[1,3,192,192]{3,2,1,0:T(8,128)(2,1)S(1)} %copy-done.169), channel_id=4, replica_groups=mesh['section'=2,'ctx'=4,'tp'=4] {'ctx'}, dimensions={2}, use_global_device_ids=true | all-gather | bytes 1105920 | tf_op jit(solution)/shard_map/all_gather | solution.py:200
  78.8 25.8 %all-gather.3 = bf16[1,192,768]{1,0,2:T(2,128)(2,1)} all-gather(bf16[1,192,192]{1,0,2:T(2,128)(2,1)S(1)} %copy.223), channel_id=5, replica_groups=mesh['section'=2,'ctx'=4,'tp'=4] {'ctx'}, dimensions={2}, use_global_device_ids=true | all-gather | bytes 368640 | tf_op jit(solution)/shard_map/all_gather | solution.py:201
  108.4 13.2 all-gather.24.cloned.1.call-done.held_ref
  140.6 26.8 %all-reduce.23.cloned.1.call-done = bf16[512,768]{1,0:T(8,128)(2,1)} async-done(((bf16[512,768]{1,0:T(8,128)(2,1)}), bf16[512,768]{1,0:T(8,128)(2,1)}) %all-reduce.23.cloned.1.call-update) | async-done | bytes 786448 | tf_op jit(solution)/shard_map/psum | solution.py:257
  169.5 29.9 %all-gather.38.cloned.1.call-done = bf16[1,768,768]{2,1,0:T(8,128)(2,1)} async-done(((bf16[1,192,768]{2,1,0:T(8,128)(2,1)}), bf16[1,768,768]{2,1,0:T(8,128)(2,1)}) %all-gather.38.cloned.1.call-update) | async-done | bytes 1179664 | tf_op jit(solution)/shard_map/all_gather | solution.py:202
  206.8 23.7 %all-gather.40.cloned.1.call-done = bf16[1,768,768]{1,2,0:T(8,128)(2,1)} async-done(((bf16[1,768,192]{1,2,0:T(8,128)(2,1)}), bf16[1,768,768]{1,2,0:T(8,128)(2,1)}) %all-gather.40.cloned.1.call-update) | async-done | bytes 1179664 | tf_op jit(solution)/shard_map/all_gather | solution.py:203
  233.8 27.3 %reduce-scatter.18.cloned.1.call-done = bf16[3,1,64,768]{3,2,0,1:T(8,128)(2,1)} async-done(((bf16[3,4,64,768]{3,2,0,1:T(8,128)(2,1)}), bf16[3,1,64,768]{3,2,0,1:T(8,128)(2,1)}) %reduce-scatter.18.cloned.1.call-update) | async-done | bytes 294928 | tf_op jit(solution)/shard_map/reduce_scatter | solution.py:236
  261.3 35.7 %all-reduce.25.cloned.1.call-done = bf16[512,768]{1,0:T(8,128)(2,1)} async-done(((bf16[512,768]{1,0:T(8,128)(2,1)}), bf16[512,768]{1,0:T(8,128)(2,1)}) %all-reduce.25.cloned.1.call-update) | async-done | bytes 786448 | tf_op jit(solution)/shard_map/psum | solution.py:257
  303.2 13.0 all-gather.42.cloned.1.call-done
  326.8 38.2 %all-gather.26.cloned.1.call-done.held_ref = bf16[2048,384]{1,0:T(8,128)(2,1)} async-done(((bf16[512,384]{1,0:T(8,128)(2,1)}), bf16[2048,384]{1,0:T(8,128)(2,1)}) %all-gather.26.cloned.1.call-update) | async-done | bytes 1572880 | tf_op jit(solution)/shard_map/all_gather | solution.py:270
  375.7 33.2 %all-reduce.27.cloned.1.call-done = bf16[512,768]{1,0:T(8,128)(2,1)} async-done(((bf16[512,768]{1,0:T(8,128)(2,1)}), bf16[512,768]{1,0:T(8,128)(2,1)}) %all-reduce.27.cloned.1.call-update) | async-done | bytes 786448 | tf_op jit(solution)/shard_map/psum | solution.py:257
  420.0 34.8 %all-reduce.29.cloned.1.call-done = bf16[512,768]{1,0:T(8,128)(2,1)} async-done(((bf16[512,768]{1,0:T(8,128)(2,1)}), bf16[512,768]{1,0:T(8,128)(2,1)}) %all-reduce.29.cloned.1.call-update) | async-done | bytes 786448 | tf_op jit(solution)/shard_map/psum | solution.py:257
  461.2 15.9 collective-permute-done.1
  482.2 38.3 %all-gather.28.cloned.1.call-done.held_ref = bf16[2048,384]{1,0:T(8,128)(2,1)} async-done(((bf16[512,384]{1,0:T(8,128)(2,1)}), bf16[2048,384]{1,0:T(8,128)(2,1)}) %all-gather.28.cloned.1.call-update) | async-done | bytes 1572880 | tf_op jit(solution)/shard_map/all_gather | solution.py:270
  530.9 33.4 %all-reduce.31.cloned.1.call-done = bf16[512,768]{1,0:T(8,128)(2,1)} async-done(((bf16[512,768]{1,0:T(8,128)(2,1)}), bf16[512,768]{1,0:T(8,128)(2,1)}) %all-reduce.31.cloned.1.call-update) | async-done | bytes 786448 | tf_op jit(solution)/shard_map/psum | solution.py:257
  575.4 34.8 %all-reduce.33.cloned.1.call-done = bf16[512,768]{1,0:T(8,128)(2,1)} async-done(((bf16[512,768]{1,0:T(8,128)(2,1)}), bf16[512,768]{1,0:T(8,128)(2,1)}) %all-reduce.33.cloned.1.call-update) | async-done | bytes 786448 | tf_op jit(solution)/shard_map/psum | solution.py:257
  616.2 15.9 collective-permute-done.2
  640.8 37.1 %all-gather.30.cloned.1.call-done.held_ref = bf16[2048,384]{1,0:T(8,128)(2,1)} async-done(((bf16[512,384]{1,0:T(8,128)(2,1)}), bf16[2048,384]{1,0:T(8,128)(2,1)}) %all-gather.30.cloned.1.call-update) | async-done | bytes 1572880 | tf_op jit(solution)/shard_map/all_gather | solution.py:270
  688.4 33.4 %all-reduce.35.cloned.1.call-done = bf16[512,768]{1,0:T(8,128)(2,1)} async-done(((bf16[512,768]{1,0:T(8,128)(2,1)}), bf16[512,768]{1,0:T(8,128)(2,1)}) %all-reduce.35.cloned.1.call-update) | async-done | bytes 786448 | tf_op jit(solution)/shard_map/psum | solution.py:257
  733.0 34.8 %all-reduce.37.cloned.1.call-done = bf16[512,768]{1,0:T(8,128)(2,1)} async-done(((bf16[512,768]{1,0:T(8,128)(2,1)}), bf16[512,768]{1,0:T(8,128)(2,1)}) %all-reduce.37.cloned.1.call-update) | async-done | bytes 786448 | tf_op jit(solution)/shard_map/psum | solution.py:257
  774.1 15.9 collective-permute-done.3
  795.0 37.1 %all-gather.32.cloned.1.call-done.held_ref = bf16[2048,384]{1,0:T(8,128)(2,1)} async-done(((bf16[512,384]{1,0:T(8,128)(2,1)}), bf16[2048,384]{1,0:T(8,128)(2,1)}) %all-gather.32.cloned.1.call-update) | async-done | bytes 1572880 | tf_op jit(solution)/shard_map/all_gather | solution.py:270
  842.8 33.2 %all-reduce.39.cloned.1.call-done = bf16[512,768]{1,0:T(8,128)(2,1)} async-done(((bf16[512,768]{1,0:T(8,128)(2,1)}), bf16[512,768]{1,0:T(8,128)(2,1)}) %all-reduce.39.cloned.1.call-update) | async-done | bytes 786448 | tf_op jit(solution)/shard_map/psum | solution.py:257
  889.8 35.4 %all-reduce.41.cloned.1.call-done = bf16[512,768]{1,0:T(8,128)(2,1)} async-done(((bf16[512,768]{1,0:T(8,128)(2,1)}), bf16[512,768]{1,0:T(8,128)(2,1)}) %all-reduce.41.cloned.1.call-update) | async-done | bytes 786448 | tf_op jit(solution)/shard_map/psum | solution.py:257
  946.3 36.2 %reduce-scatter.20.cloned.1.call-done = bf16[512,384]{1,0:T(8,128)(2,1)} async-done(((bf16[2048,384]{1,0:T(8,128)(2,1)}), bf16[512,384]{1,0:T(8,128)(2,1)}) %reduce-scatter.20.cloned.1.call-update) | async-done | bytes 393232 | tf_op jit(solution)/shard_map/reduce_scatter | solution.py:333
  985.9 33.7 %all-reduce.43.cloned.1.call-done = bf16[512,768]{1,0:T(8,128)(2,1)} async-done(((bf16[512,768]{1,0:T(8,128)(2,1)}), bf16[512,768]{1,0:T(8,128)(2,1)}) %all-reduce.43.cloned.1.call-update) | async-done | bytes 786448 | tf_op jit(solution)/shard_map/psum | solution.py:257
  1026.0 18.6 collective-permute-done.4
  1050.9 33.5 %all-reduce.45.cloned.1.call-done = bf16[512,768]{1,0:T(8,128)(2,1)} async-done(((bf16[512,768]{1,0:T(8,128)(2,1)}), bf16[512,768]{1,0:T(8,128)(2,1)}) %all-reduce.45.cloned.1.call-update) | async-done | bytes 786448 | tf_op jit(solution)/shard_map/psum | solution.py:257
  1105.2 35.4 %reduce-scatter.22.cloned.1.call-done = bf16[512,384]{1,0:T(8,128)(2,1)} async-done(((bf16[2048,384]{1,0:T(8,128)(2,1)}), bf16[512,384]{1,0:T(8,128)(2,1)}) %reduce-scatter.22.cloned.1.call-update) | async-done | bytes 393232 | tf_op jit(solution)/shard_map/reduce_scatter | solution.py:333
  1144.1 33.7 %all-reduce.47.cloned.1.call-done = bf16[512,768]{1,0:T(8,128)(2,1)} async-done(((bf16[512,768]{1,0:T(8,128)(2,1)}), bf16[512,768]{1,0:T(8,128)(2,1)}) %all-reduce.47.cloned.1.call-update) | async-done | bytes 786448 | tf_op jit(solution)/shard_map/psum | solution.py:257
  1186.0 18.2 collective-permute-done.5
  1210.5 33.7 %all-reduce.49.cloned.1.call-done = bf16[512,768]{1,0:T(8,128)(2,1)} async-done(((bf16[512,768]{1,0:T(8,128)(2,1)}), bf16[512,768]{1,0:T(8,128)(2,1)}) %all-reduce.49.cloned.1.call-update) | async-done | bytes 786448 | tf_op jit(solution)/shard_map/psum | solution.py:257
  1265.0 35.4 %reduce-scatter.24.cloned.1.call-done = bf16[512,384]{1,0:T(8,128)(2,1)} async-done(((bf16[2048,384]{1,0:T(8,128)(2,1)}), bf16[512,384]{1,0:T(8,128)(2,1)}) %reduce-scatter.24.cloned.1.call-update) | async-done | bytes 393232 | tf_op jit(solution)/shard_map/reduce_scatter | solution.py:333
  1304.1 33.5 %all-reduce.51.cloned.1.call-done = bf16[512,768]{1,0:T(8,128)(2,1)} async-done(((bf16[512,768]{1,0:T(8,128)(2,1)}), bf16[512,768]{1,0:T(8,128)(2,1)}) %all-reduce.51.cloned.1.call-update) | async-done | bytes 786448 | tf_op jit(solution)/shard_map/psum | solution.py:257
  1344.8 18.6 collective-permute-done.6
  1369.7 33.7 %all-reduce.53.cloned.1.call-done = bf16[512,768]{1,0:T(8,128)(2,1)} async-done(((bf16[512,768]{1,0:T(8,128)(2,1)}), bf16[512,768]{1,0:T(8,128)(2,1)}) %all-reduce.53.cloned.1.call-update) | async-done | bytes 786448 | tf_op jit(solution)/shard_map/psum | solution.py:257
  1423.4 35.4 %reduce-scatter.26.cloned.1.call-done = bf16[512,384]{1,0:T(8,128)(2,1)} async-done(((bf16[2048,384]{1,0:T(8,128)(2,1)}), bf16[512,384]{1,0:T(8,128)(2,1)}) %reduce-scatter.26.cloned.1.call-update) | async-done | bytes 393232 | tf_op jit(solution)/shard_map/reduce_scatter | solution.py:333
  1462.3 33.7 %all-reduce.55.cloned.1.call-done = bf16[512,768]{1,0:T(8,128)(2,1)} async-done(((bf16[512,768]{1,0:T(8,128)(2,1)}), bf16[512,768]{1,0:T(8,128)(2,1)}) %all-reduce.55.cloned.1.call-update) | async-done | bytes 786448 | tf_op jit(solution)/shard_map/psum | solution.py:257
  1503.7 18.6 collective-permute-done.7
  1528.2 33.3 %all-reduce.57.cloned.1.call-done = bf16[512,768]{1,0:T(8,128)(2,1)} async-done(((bf16[512,768]{1,0:T(8,128)(2,1)}), bf16[512,768]{1,0:T(8,128)(2,1)}) %all-reduce.57.cloned.1.call-update) | async-done | bytes 786448 | tf_op jit(solution)/shard_map/psum | solution.py:257
  1589.8 32.2 %reduce-scatter.28.cloned.1.call-done = bf16[512,384]{1,0:T(8,128)(2,1)} async-done(((bf16[2048,384]{1,0:T(8,128)(2,1)}), bf16[512,384]{1,0:T(8,128)(2,1)}) %reduce-scatter.28.cloned.1.call-update) | async-done | bytes 393232 | tf_op jit(solution)/shard_map/reduce_scatter | solution.py:333
  1638.3 29.9 %all-reduce.59.cloned.1.call-done = (bf16[512,768]{1,0:T(8,128)(2,1)}, bf16[512,768]{1,0:T(8,128)(2,1)}) async-done(((bf16[512,768]{1,0:T(8,128)(2,1)}, bf16[512,768]{1,0:T(8,128)(2,1)}), (bf16[512,768]{1,0:T(8,128)(2,1)}, bf16[512,768]{1,0:T(8,128)(2,1)})) %all-reduce.59.cloned.1.call-update) | async-done | bytes 1572880 | tf_op jit(solution)/shard_map/psum | solution.py:257
  1695.3 12.3 all-gather.46.cloned.1.call-done
  1780.8 24.4 %reduce-scatter.32.cloned.1.call-done = bf16[768,192]{0,1:T(8,128)(2,1)} async-done(((bf16[768,768]{0,1:T(8,128)(2,1)}), bf16[768,192]{0,1:T(8,128)(2,1)}) %reduce-scatter.32.cloned.1.call-update) | async-done | bytes 294928 | tf_op jit(solution)/shard_map/reduce_scatter | solution.py:421
  1807.1 28.3 %reduce-scatter.30.cloned.1.call-done = bf16[192,768]{1,0:T(8,128)(2,1)} async-done(((bf16[768,768]{1,0:T(8,128)(2,1)}), bf16[192,768]{1,0:T(8,128)(2,1)}) %reduce-scatter.30.cloned.1.call-update) | async-done | bytes 294928 | tf_op jit(solution)/shard_map/reduce_scatter | solution.py:421
  1844.4 16.4 all-reduce.1
  1871.3 18.4 all-gather.8
  (1065 shorter events, 571.1 us)
Async XLA Ops:
  7.2 60.5 %reduce-scatter.16.cloned.1.call-start = ((), (), s32[]{:S(2)}) async-start(), calls=%async_computation.11 | async-start | bytes 491520 | tf_op jit(solution)/shard_map/reduce_scatter | solution.py:236
  23.6 98.0 %all-gather.24.cloned.1.call-start = ((), (), s32[]{:S(2)}) async-start(), calls=%async_computation.12 | async-start | bytes 1966080 | tf_op jit(solution)/shard_map/all_gather | solution.py:270
  78.5 88.9 %all-reduce.23.cloned.1.call-start = ((), (), s32[]{:S(2)}) async-start(), calls=%async_computation.13 | async-start | bytes 1572864 | tf_op jit(solution)/shard_map/psum | solution.py:257
  132.7 66.8 %all-gather.38.cloned.1.call-start = ((), (), s32[]{:S(2)}) async-start(), calls=%async_computation.45 | async-start | bytes 1474560 | tf_op jit(solution)/shard_map/all_gather | solution.py:202
  133.2 97.3 %all-gather.40.cloned.1.call-start = ((), (), s32[]{:S(2)}) async-start(), calls=%async_computation.46 | async-start | bytes 1474560 | tf_op jit(solution)/shard_map/all_gather | solution.py:203
  133.8 127.3 %reduce-scatter.18.cloned.1.call-start = ((), (), s32[]{:S(2)}) async-start(), calls=%async_computation.15 | async-start | bytes 1474560 | tf_op jit(solution)/shard_map/reduce_scatter | solution.py:236
  139.3 157.7 %all-reduce.25.cloned.1.call-start = ((), (), s32[]{:S(2)}) async-start(), calls=%async_computation.14 | async-start | bytes 1572864 | tf_op jit(solution)/shard_map/psum | solution.py:257
  233.8 82.4 %all-gather.42.cloned.1.call-start = ((), (), s32[]{:S(2)}) async-start(), calls=%async_computation.47 | async-start | bytes 1474560 | tf_op jit(solution)/shard_map/all_gather | solution.py:237
  261.1 103.8 %all-gather.26.cloned.1.call-start = ((), (), s32[]{:S(2)}) async-start(), calls=%async_computation.16 | async-start | bytes 1966080 | tf_op jit(solution)/shard_map/all_gather | solution.py:270
  299.7 19.6 %collective-permute-start = (bf16[512,768]{1,0:T(8,128)(2,1)}, bf16[512,768]{1,0:T(8,128)(2,1)S(1)}, u32[]{:S(2)}, u32[]{:S(2)}) collective-permute-start(bf16[512,768]{1,0:T(8,128)(2,1)} %add_convert_fusion.20), channel_id=1, source_target_pairs={{0,16},{1,17},{2,18},{3,19},{4,20},{5,21},{6,22},{7,23},{8,24},{9,... | collective-permute-start | bytes 2359304 | tf_op jit(solution)/shard_map/ppermute | solution.py:18
  325.2 83.7 %all-reduce.27.cloned.1.call-start = ((), (), s32[]{:S(2)}) async-start(), calls=%async_computation.17 | async-start | bytes 1572864 | tf_op jit(solution)/shard_map/psum | solution.py:257
  375.2 79.6 %all-reduce.29.cloned.1.call-start = ((), (), s32[]{:S(2)}) async-start(), calls=%async_computation.18 | async-start | bytes 1572864 | tf_op jit(solution)/shard_map/psum | solution.py:257
  420.0 100.5 %all-gather.28.cloned.1.call-start = ((), (), s32[]{:S(2)}) async-start(), calls=%async_computation.19 | async-start | bytes 1966080 | tf_op jit(solution)/shard_map/all_gather | solution.py:270
  481.8 82.6 %all-reduce.31.cloned.1.call-start = ((), (), s32[]{:S(2)}) async-start(), calls=%async_computation.20 | async-start | bytes 1572864 | tf_op jit(solution)/shard_map/psum | solution.py:257
  530.7 79.5 %all-reduce.33.cloned.1.call-start = ((), (), s32[]{:S(2)}) async-start(), calls=%async_computation.21 | async-start | bytes 1572864 | tf_op jit(solution)/shard_map/psum | solution.py:257
  575.4 102.4 %all-gather.30.cloned.1.call-start = ((), (), s32[]{:S(2)}) async-start(), calls=%async_computation.22 | async-start | bytes 1966080 | tf_op jit(solution)/shard_map/all_gather | solution.py:270
  639.1 82.7 %all-reduce.35.cloned.1.call-start = ((), (), s32[]{:S(2)}) async-start(), calls=%async_computation.23 | async-start | bytes 1572864 | tf_op jit(solution)/shard_map/psum | solution.py:257
  688.1 79.6 %all-reduce.37.cloned.1.call-start = ((), (), s32[]{:S(2)}) async-start(), calls=%async_computation.24 | async-start | bytes 1572864 | tf_op jit(solution)/shard_map/psum | solution.py:257
  733.0 99.1 %all-gather.32.cloned.1.call-start = ((), (), s32[]{:S(2)}) async-start(), calls=%async_computation.25 | async-start | bytes 1966080 | tf_op jit(solution)/shard_map/all_gather | solution.py:270
  770.8 19.2 collective-permute-start.3
  793.4 82.7 %all-reduce.39.cloned.1.call-start = ((), (), s32[]{:S(2)}) async-start(), calls=%async_computation.26 | async-start | bytes 1572864 | tf_op jit(solution)/shard_map/psum | solution.py:257
  842.4 82.9 %all-reduce.41.cloned.1.call-start = ((), (), s32[]{:S(2)}) async-start(), calls=%async_computation.28 | async-start | bytes 1572864 | tf_op jit(solution)/shard_map/psum | solution.py:257
  888.6 93.9 %reduce-scatter.20.cloned.1.call-start = ((), (), s32[]{:S(2)}) async-start(), calls=%async_computation.29 | async-start | bytes 1966080 | tf_op jit(solution)/shard_map/reduce_scatter | solution.py:333
  946.3 73.3 %all-reduce.43.cloned.1.call-start = ((), (), s32[]{:S(2)}) async-start(), calls=%async_computation.30 | async-start | bytes 1572864 | tf_op jit(solution)/shard_map/psum | solution.py:257
  985.9 98.6 %all-reduce.45.cloned.1.call-start = ((), (), s32[]{:S(2)}) async-start(), calls=%async_computation.31 | async-start | bytes 1572864 | tf_op jit(solution)/shard_map/psum | solution.py:257
  1024.3 20.3 %collective-permute-start.4 = (bf16[512,768]{1,0:T(8,128)(2,1)S(1)}, bf16[512,768]{1,0:T(8,128)(2,1)S(1)}, u32[]{:S(2)}, u32[]{:S(2)}) collective-permute-start(bf16[512,768]{1,0:T(8,128)(2,1)S(1)} %fusion.64), channel_id=1, source_target_pairs={{16,0},{17,1},{18,2},{19,3},{20,4},{21,5},{22,6},{23,7},{24,8},{25... | collective-permute-start | bytes 2359304 | tf_op jit(solution)/shard_map/ppermute | solution.py:18
  1049.8 90.8 %reduce-scatter.22.cloned.1.call-start = ((), (), s32[]{:S(2)}) async-start(), calls=%async_computation.32 | async-start | bytes 1966080 | tf_op jit(solution)/shard_map/reduce_scatter | solution.py:333
  1105.1 72.6 %all-reduce.47.cloned.1.call-start = ((), (), s32[]{:S(2)}) async-start(), calls=%async_computation.33 | async-start | bytes 1572864 | tf_op jit(solution)/shard_map/psum | solution.py:257
  1144.0 100.2 %all-reduce.49.cloned.1.call-start = ((), (), s32[]{:S(2)}) async-start(), calls=%async_computation.34 | async-start | bytes 1572864 | tf_op jit(solution)/shard_map/psum | solution.py:257
  1183.9 20.2 %collective-permute-start.5 = (bf16[512,768]{1,0:T(8,128)(2,1)S(1)}, bf16[512,768]{1,0:T(8,128)(2,1)S(1)}, u32[]{:S(2)}, u32[]{:S(2)}) collective-permute-start(bf16[512,768]{1,0:T(8,128)(2,1)S(1)} %get-tuple-element.174), channel_id=1, source_target_pairs={{16,0},{17,1},{18,2},{19,3},{20,4},{21,5},{22,6},{23,7},{24,8},{25... | collective-permute-start | bytes 2359304 | tf_op jit(solution)/shard_map/ppermute | solution.py:18
  1209.5 90.9 %reduce-scatter.24.cloned.1.call-start = ((), (), s32[]{:S(2)}) async-start(), calls=%async_computation.35 | async-start | bytes 1966080 | tf_op jit(solution)/shard_map/reduce_scatter | solution.py:333
  1264.9 72.6 %all-reduce.51.cloned.1.call-start = ((), (), s32[]{:S(2)}) async-start(), calls=%async_computation.36 | async-start | bytes 1572864 | tf_op jit(solution)/shard_map/psum | solution.py:257
  1303.8 99.6 %all-reduce.53.cloned.1.call-start = ((), (), s32[]{:S(2)}) async-start(), calls=%async_computation.37 | async-start | bytes 1572864 | tf_op jit(solution)/shard_map/psum | solution.py:257
  1343.3 20.1 %collective-permute-start.6 = (bf16[512,768]{1,0:T(8,128)(2,1)S(1)}, bf16[512,768]{1,0:T(8,128)(2,1)S(1)}, u32[]{:S(2)}, u32[]{:S(2)}) collective-permute-start(bf16[512,768]{1,0:T(8,128)(2,1)S(1)} %get-tuple-element.172), channel_id=1, source_target_pairs={{16,0},{17,1},{18,2},{19,3},{20,4},{21,5},{22,6},{23,7},{24,8},{25... | collective-permute-start | bytes 2359304 | tf_op jit(solution)/shard_map/ppermute | solution.py:18
  1368.7 90.2 %reduce-scatter.26.cloned.1.call-start = ((), (), s32[]{:S(2)}) async-start(), calls=%async_computation.38 | async-start | bytes 1966080 | tf_op jit(solution)/shard_map/reduce_scatter | solution.py:333
  1423.3 72.7 %all-reduce.55.cloned.1.call-start = ((), (), s32[]{:S(2)}) async-start(), calls=%async_computation.39 | async-start | bytes 1572864 | tf_op jit(solution)/shard_map/psum | solution.py:257
  1462.3 99.2 %all-reduce.57.cloned.1.call-start = ((), (), s32[]{:S(2)}) async-start(), calls=%async_computation.40 | async-start | bytes 1572864 | tf_op jit(solution)/shard_map/psum | solution.py:257
  1502.4 19.9 %collective-permute-start.7 = (bf16[512,768]{1,0:T(8,128)(2,1)S(1)}, bf16[512,768]{1,0:T(8,128)(2,1)S(1)}, u32[]{:S(2)}, u32[]{:S(2)}) collective-permute-start(bf16[512,768]{1,0:T(8,128)(2,1)S(1)} %get-tuple-element.170), channel_id=1, source_target_pairs={{16,0},{17,1},{18,2},{19,3},{20,4},{21,5},{22,6},{23,7},{24,8},{25... | collective-permute-start | bytes 2359304 | tf_op jit(solution)/shard_map/ppermute | solution.py:18
  1526.8 95.3 %reduce-scatter.28.cloned.1.call-start = ((), (), s32[]{:S(2)}) async-start(), calls=%async_computation.41 | async-start | bytes 1966080 | tf_op jit(solution)/shard_map/reduce_scatter | solution.py:333
  1586.6 81.7 %all-reduce.59.cloned.1.call-start = ((), (), s32[]{:S(2)}) async-start(), calls=%async_computation.52 | async-start | bytes 3145728 | tf_op jit(solution)/shard_map/psum | solution.py:257
  1626.0 81.6 %all-gather.46.cloned.1.call-start = ((), (), s32[]{:S(2)}) async-start(), calls=%async_computation.49 | async-start | bytes 1966080 | tf_op jit(solution)/shard_map/all_gather | solution.py:243
  1630.6 143.2 %reduce-scatter.36.cloned.1.call-start = ((), (), s32[]{:S(2)}) async-start(), calls=%async_computation.51 | async-start | bytes 491520
  1638.1 137.4 %all-gather.44.cloned.1.call-start = ((), (), s32[]{:S(2)}) async-start(), calls=%async_computation.48 | async-start | bytes 2621440 | tf_op jit(solution)/shard_map/all_gather | solution.py:243
  1674.4 130.9 %reduce-scatter.32.cloned.1.call-start = ((), (), s32[]{:S(2)}) async-start(), calls=%async_computation.44 | async-start | bytes 1474560 | tf_op jit(solution)/shard_map/reduce_scatter | solution.py:421
  1683.1 152.2 %reduce-scatter.30.cloned.1.call-start = ((), (), s32[]{:S(2)}) async-start(), calls=%async_computation.43 | async-start | bytes 1474560 | tf_op jit(solution)/shard_map/reduce_scatter | solution.py:421
  1695.1 205.2 %all-gather.36.cloned.1.call-start = ((), (), s32[]{:S(2)}) async-start(), calls=%async_computation.42 | async-start | bytes 2949120 | tf_op jit(solution)/shard_map/all_gather | solution.py:247
  1712.3 203.2 %reduce-scatter.34.cloned.1.call-start = ((), (), s32[]{:S(2)}) async-start(), calls=%async_computation.50 | async-start | bytes 1228800
  1742.6 181.3 %all-gather.34.cloned.1.call-start = ((), (), s32[]{:S(2)}) async-start(), calls=%async_computation.27 | async-start | bytes 3932160 | tf_op jit(solution)/shard_map/all_gather | solution.py:247
  (292 other events, 11138.0 us)
Sparse Core Ops, SparseCore 0:
  23.7 23.4 reduce-scatter.15
  78.6 42.9 all-gather.23
  132.8 34.5 all-reduce.22
  168.9 30.4 all-gather.37
  200.9 29.5 all-gather.39
  232.8 28.2 reduce-scatter.17
  263.6 33.3 all-reduce.24
  298.6 17.4 all-gather.41
  325.4 39.5 all-gather.25
  375.4 33.5 all-reduce.26
  420.1 34.6 all-reduce.28
  481.9 38.5 all-gather.27
  530.8 33.4 all-reduce.30
  575.5 34.6 all-reduce.32
  639.2 38.5 all-gather.29
  688.3 33.4 all-reduce.34
  733.1 34.6 all-reduce.36
  793.5 38.5 all-gather.31
  842.5 33.4 all-reduce.38
  888.7 36.4 all-reduce.40
  946.4 36.0 reduce-scatter.19
  986.0 33.5 all-reduce.42
  1050.0 34.4 all-reduce.44
  1105.3 35.3 reduce-scatter.21
  1144.2 33.5 all-reduce.46
  1209.6 34.5 all-reduce.48
  1265.0 35.3 reduce-scatter.23
  1304.0 33.5 all-reduce.50
  1368.8 34.5 all-reduce.52
  1423.4 35.3 reduce-scatter.25
  1462.4 33.5 all-reduce.54
  1526.9 34.5 all-reduce.56
  1586.7 35.3 reduce-scatter.27
  1626.2 42.0 all-reduce.58
  1670.5 37.1 all-gather.45
  1709.9 19.5 reduce-scatter.35
  1730.9 44.0 all-gather.43
  1777.3 27.8 reduce-scatter.31
  1807.4 27.8 reduce-scatter.29
  1837.5 22.7 all-gather.35
  1862.6 32.2 reduce-scatter.33
  1896.6 27.2 all-gather.33

commit v2 on v1

--- a/solution.py
+++ b/solution.py
@@ -253,8 +253,31 @@
     entry_rest = spread(entering, 1, micro_count)
     entry_rows = [entry_first[0]] + [entry_rest[i] for i in range(micro_count - 1)]
 
+    def swap(rows, distance):
+        return lax.ppermute(rows, "tp", [(i, i ^ distance) for i in range(tp_count)])
+
+    def joined(rows):
+        other = swap(rows, 1)
+        even = tp_index % 2 == 0
+        return jnp.concatenate([jnp.where(even, rows, other), jnp.where(even, other, rows)], axis=0)
+
+    def pair_half(rows, place):
+        return jnp.where(place == 0, rows[:half], rows[half:])
+
     def tp_total(partial_rows):
-        return lax.psum(partial_rows.astype(jnp.bfloat16), "tp").astype(jnp.float32)
+        rows = partial_rows.astype(jnp.bfloat16)
+        place = tp_index % 2
+        total = pair_half(rows, place).astype(jnp.float32)
+        total = total + swap(pair_half(rows, 1 - place), 1).astype(jnp.float32)
+        distance = 2
+        while distance < tp_count:
+            low = total.astype(jnp.bfloat16)
+            total = low.astype(jnp.float32) + swap(low, distance).astype(jnp.float32)
+            distance *= 2
+        return joined(total.astype(jnp.bfloat16)).astype(jnp.float32)
+
+    def to_section(rows, distance):
+        return joined(from_behind(pair_half(rows, tp_index % 2), "section", distance))
 
     def layer_forward(current):
         residual = current.astype(jnp.float32)
@@ -382,7 +405,7 @@
         produced.append(output_low)
         memory.append(kept)
         if tick_index < micro_count:
-            incoming = from_behind(output_low, "section", 1)
+            incoming = to_section(output_low, 1)
     acts = restore(
         jnp.stack(
             [
@@ -405,7 +428,7 @@
         totals = grads if totals is None else jax.tree.map(jnp.add, totals, grads)
         returned.append(entry_low)
         if tick_index < micro_count:
-            returning = from_behind(entry_low, "section", -1)
+            returning = to_section(entry_low, -1)
     grad_inputs = [
         jnp.where(section_index == 0, returned[micro_count - i], returned[micro_count - 1 - i])
         for i in range(micro_count)

time: 1960 us -> 1450 us (0.74)
  waiting for transfers between devices: 1260 us -> 709 us
  starting transfers between devices: 24.1 us -> 58.6 us
    psum x19 -> x0, waiting for transfers between devices: 634 us -> none  [tp_total(): return lax.psum(partial_rows.astype(jnp.bfloat16), 'tp').astype(jnp.float32)]
    ppermute x0 -> x68, waiting for transfers between devices: none -> 239 us  [swap(): lax.ppermute(rows, 'tp', [(i, i ^ distance) for i in range(tp_count)])]
    reduce_scatter x2, waiting for transfers between devices: 52.7 us -> 9.53 us  [owned(): lax.psum_scatter(total.astype(jnp.bfloat16), 'ctx', scatter_dimension=dim...]
    ppermute x8, waiting for transfers between devices: 123 us -> 80.3 us  [from_behind(): return lax.ppermute(block, axis, route)]
    ppermute x0 -> x68, starting transfers between devices: none -> 34.9 us  [swap(): lax.ppermute(rows, 'tp', [(i, i ^ distance) for i in range(tp_count)])]
    reduce_scatter x5, waiting for transfers between devices: 175 us -> 141 us  [layer_backward(): lax.psum_scatter(grad_held.astype(jnp.bfloat16), 'ctx', scatter_dimension...]
    select_n x0 -> x62, other arithmetic: none -> 32.5 us  [the longest x4 17.4 us: local(): jnp.where(section_index == 0, returned[micro_count - i], returned[micro_c...]
    all_gather x1, waiting for transfers between devices: 29.9 us -> 0.59 us  [local(): expand_weight = lax.all_gather(up_weight[0], 'ctx', axis=0, tiled=True)]
  transfers between devices with their start and end apart: 50 -> 99, of which waited for: 45 -> 82; matrix products, arithmetic and copies ran while one was open for 10% -> 16% of each run, Pallas kernels for 0% -> 1%
where the time goes in v2:
time: 1450 us; the launch traced here: 1440 us
  waiting for transfers between devices  709 us (49%)
  other arithmetic  156 us (11%)
  matrix products  149 us (10%)
  local copies, waits for them, and re-layouts  143 us (10%)
  blocking collectives  118 us (8%)
  Pallas kernels  81 us (6%)
  starting transfers between devices  58.6 us (4%)
  between operations  22.1 us (2%)
    ppermute x68, waiting for transfers between devices, swap(): lax.ppermute(rows, 'tp', [(i, i ^ distance) for i in range(tp_count)])  239 us
    all_gather x5, waiting for transfers between devices, layer_forward(): held = lax.all_gather(held_part, 'ctx', axis=0, tiled=True)  154 us
    reduce_scatter x5, waiting for transfers between devices, layer_backward(): lax.psum_scatter(grad_held.astype(jnp.bfloat16), 'ctx', scatter_dimension...  141 us
    dot_general x90, matrix products, contract(): lax.dot_general(left, right, (((left_dim,), (right_dim,)), ((), ())), pre...  132 us
    unnamed x1023, local copies, waits for them, and re-layouts  80.8 us
    ppermute x8, waiting for transfers between devices, from_behind(): return lax.ppermute(block, axis, route)  80.3 us
    pallas_call x5, Pallas kernels, attend_back(): pl.pallas_call(partial(attend_back_kernel, heads), grid=(rows // block,),...  43.7 us
    pallas_call x5, Pallas kernels, attend(): pl.pallas_call(partial(attend_kernel, heads), grid=(rows // block,), in_s...  37.3 us
  transfers between devices with their start and end apart: 99, of which 82 were waited for; matrix products, arithmetic and copies ran while one was open for 16% of the time, Pallas kernels for 1%

profile of v2, /device:TPU:0, one launch (start us, length us, event | category | flops | bytes accessed | tf_op | source)
XLA Modules:
  0.0 1437.7 jit_solution(9240672602721095222)
XLA Ops:
  26.2 20.4 %all-reduce = bf16[5760]{0:T(1024)(128)(2,1)S(1)} all-reduce(bf16[5760]{0:T(1024)(128)(2,1)S(1)} %dynamic-update-slice), channel_id=3, replica_groups=mesh['section'=2,'ctx'=4,'tp'=4] {'ctx'}, use_global_device_ids=true, to_apply=%add | all-reduce | flops 5760 | bytes 23040
  47.5 20.7 %all-gather.2 = bf16[1,3,768,192]{3,2,1,0:T(8,128)(2,1)S(1)} all-gather(bf16[1,3,192,192]{3,2,1,0:T(8,128)(2,1)S(1)} %copy-done.297), channel_id=4, replica_groups=mesh['section'=2,'ctx'=4,'tp'=4] {'ctx'}, dimensions={2}, use_global_device_ids=true | all-gather | bytes 1105920 | tf_op jit(solution)/shard_map/all_gather | solution.py:200
  81.3 28.0 %all-gather.3 = bf16[1,192,768]{1,0,2:T(2,128)(2,1)} all-gather(bf16[1,192,192]{1,0,2:T(2,128)(2,1)S(1)} %copy.223), channel_id=5, replica_groups=mesh['section'=2,'ctx'=4,'tp'=4] {'ctx'}, dimensions={2}, use_global_device_ids=true | all-gather | bytes 368640 | tf_op jit(solution)/shard_map/all_gather | solution.py:201
  113.1 11.0 all-gather.24.cloned.1.call-done.held_ref
  163.9 23.7 %all-gather.40.cloned.1.call-done = bf16[1,768,768]{1,2,0:T(8,128)(2,1)} async-done(((bf16[1,768,192]{1,2,0:T(8,128)(2,1)}), bf16[1,768,768]{1,2,0:T(8,128)(2,1)}) %all-gather.40.cloned.1.call-update) | async-done | bytes 1179664 | tf_op jit(solution)/shard_map/all_gather | solution.py:203
  194.2 24.0 %reduce-scatter.18.cloned.1.call-done = bf16[3,1,64,768]{3,2,0,1:T(8,128)(2,1)} async-done(((bf16[3,4,64,768]{3,2,0,1:T(8,128)(2,1)}), bf16[3,1,64,768]{3,2,0,1:T(8,128)(2,1)}) %reduce-scatter.18.cloned.1.call-update) | async-done | bytes 294928 | tf_op jit(solution)/shard_map/reduce_scatter | solution.py:236
  249.0 36.0 %all-gather.26.cloned.1.call-done.held_ref = bf16[2048,384]{1,0:T(8,128)(2,1)} async-done(((bf16[512,384]{1,0:T(8,128)(2,1)}), bf16[2048,384]{1,0:T(8,128)(2,1)}) %all-gather.26.cloned.1.call-update) | async-done | bytes 1572880 | tf_op jit(solution)/shard_map/all_gather | solution.py:293
  297.9 9.7 collective-permute-done.9
  321.3 9.7 collective-permute-done.12
  337.6 8.6 collective-permute-done.14
  356.3 36.0 %all-gather.28.cloned.1.call-done.held_ref = bf16[2048,384]{1,0:T(8,128)(2,1)} async-done(((bf16[512,384]{1,0:T(8,128)(2,1)}), bf16[2048,384]{1,0:T(8,128)(2,1)}) %all-gather.28.cloned.1.call-update) | async-done | bytes 1572880 | tf_op jit(solution)/shard_map/all_gather | solution.py:293
  405.2 9.7 collective-permute-done.17
  430.5 9.7 collective-permute-done.20
  463.5 35.5 %all-gather.30.cloned.1.call-done.held_ref = bf16[2048,384]{1,0:T(8,128)(2,1)} async-done(((bf16[512,384]{1,0:T(8,128)(2,1)}), bf16[2048,384]{1,0:T(8,128)(2,1)}) %all-gather.30.cloned.1.call-update) | async-done | bytes 1572880 | tf_op jit(solution)/shard_map/all_gather | solution.py:293
  511.8 9.7 collective-permute-done.25
  535.2 9.7 collective-permute-done.28
  568.3 35.5 %all-gather.32.cloned.1.call-done.held_ref = bf16[2048,384]{1,0:T(8,128)(2,1)} async-done(((bf16[512,384]{1,0:T(8,128)(2,1)}), bf16[2048,384]{1,0:T(8,128)(2,1)}) %all-gather.32.cloned.1.call-update) | async-done | bytes 1572880 | tf_op jit(solution)/shard_map/all_gather | solution.py:293
  616.6 9.7 collective-permute-done.33
  641.9 9.7 collective-permute-done.39
  662.6 8.8 shard_map.191
  672.7 34.2 %reduce-scatter.20.cloned.1.call-done = bf16[512,384]{1,0:T(8,128)(2,1)} async-done(((bf16[2048,384]{1,0:T(8,128)(2,1)}), bf16[512,384]{1,0:T(8,128)(2,1)}) %reduce-scatter.20.cloned.1.call-update) | async-done | bytes 393232 | tf_op jit(solution)/shard_map/reduce_scatter | solution.py:356
  712.9 9.7 collective-permute-done.42
  728.6 11.3 collective-permute-done.44
  750.2 9.7 collective-permute-done.47
  771.1 8.7 shard_map.192
  781.4 33.3 %reduce-scatter.22.cloned.1.call-done = bf16[512,384]{1,0:T(8,128)(2,1)} async-done(((bf16[2048,384]{1,0:T(8,128)(2,1)}), bf16[512,384]{1,0:T(8,128)(2,1)}) %reduce-scatter.22.cloned.1.call-update) | async-done | bytes 393232 | tf_op jit(solution)/shard_map/reduce_scatter | solution.py:356
  822.6 9.7 collective-permute-done.50
  837.8 11.8 collective-permute-done.52
  859.8 9.7 collective-permute-done.55
  883.0 8.7 shard_map.193
  893.6 33.1 %reduce-scatter.24.cloned.1.call-done = bf16[512,384]{1,0:T(8,128)(2,1)} async-done(((bf16[2048,384]{1,0:T(8,128)(2,1)}), bf16[512,384]{1,0:T(8,128)(2,1)}) %reduce-scatter.24.cloned.1.call-update) | async-done | bytes 393232 | tf_op jit(solution)/shard_map/reduce_scatter | solution.py:356
  934.6 9.7 collective-permute-done.58
  951.0 11.8 collective-permute-done.60
  973.0 9.7 collective-permute-done.63
  996.4 8.7 shard_map.194
  1006.6 33.3 %reduce-scatter.26.cloned.1.call-done = bf16[512,384]{1,0:T(8,128)(2,1)} async-done(((bf16[2048,384]{1,0:T(8,128)(2,1)}), bf16[512,384]{1,0:T(8,128)(2,1)}) %reduce-scatter.26.cloned.1.call-update) | async-done | bytes 393232 | tf_op jit(solution)/shard_map/reduce_scatter | solution.py:356
  1046.0 9.7 collective-permute-done.66
  1061.3 11.8 collective-permute-done.68
  1082.8 9.0 collective-permute-done.71
  1109.1 8.7 shard_map.195
  1123.9 10.3 collective-permute-done.36
  1165.1 35.6 %all-gather.44.cloned.1.call-done = bf16[4,1024,192]{2,1,0:T(8,128)(2,1)} async-done(((bf16[4,256,192]{2,1,0:T(8,128)(2,1)}), bf16[4,1024,192]{2,1,0:T(8,128)(2,1)}) %all-gather.44.cloned.1.call-update) | async-done | bytes 1572880 | tf_op jit(solution)/shard_map/all_gather | solution.py:243
  1310.3 8.7 copy.269
  1344.2 9.5 reduce-scatter.30.cloned.1.call-done
  1356.8 16.7 %all-reduce.1 = bf16[4,1440]{1,0:T(4,128)(2,1)S(1)} all-reduce(bf16[4,1440]{1,0:T(4,128)(2,1)S(1)} %concatenate.687), channel_id=20, replica_groups=mesh['section'=2,'ctx'=4,'tp'=4] {'ctx'}, use_global_device_ids=true, to_apply=%region_102.103.clone | all-reduce | flops 5760 | bytes 23040
  1382.2 14.5 %all-gather.8 = bf16[4,256,192]{1,2,0:T(8,128)(2,1)S(1)} all-gather(bf16[1,256,192]{1,2,0:T(8,128)(2,1)} %copy.261), channel_id=10, replica_groups=mesh['section'=2,'ctx'=4,'tp'=4] {'ctx'}, dimensions={0}, use_global_device_ids=true | all-gather | bytes 491520 | tf_op jit(solution)/shard_map/all_gather | solution.py:243
  1398.3 11.4 all-gather.9
  1422.3 8.6 copy.270
  (1673 shorter events, 642.0 us)
Async XLA Ops:
  7.2 61.0 %reduce-scatter.16.cloned.1.call-start = ((), (), s32[]{:S(2)}) async-start(), calls=%async_computation.11 | async-start | bytes 491520 | tf_op jit(solution)/shard_map/reduce_scatter | solution.py:236
  24.1 100.0 %all-gather.24.cloned.1.call-start = ((), (), s32[]{:S(2)}) async-start(), calls=%async_computation.12 | async-start | bytes 1966080 | tf_op jit(solution)/shard_map/all_gather | solution.py:293
  79.1 77.5 %all-gather.38.cloned.1.call-start = ((), (), s32[]{:S(2)}) async-start(), calls=%async_computation.27 | async-start | bytes 1474560 | tf_op jit(solution)/shard_map/all_gather | solution.py:202
  79.8 107.8 %all-gather.40.cloned.1.call-start = ((), (), s32[]{:S(2)}) async-start(), calls=%async_computation.28 | async-start | bytes 1474560 | tf_op jit(solution)/shard_map/all_gather | solution.py:203
  80.4 137.8 %reduce-scatter.18.cloned.1.call-start = ((), (), s32[]{:S(2)}) async-start(), calls=%async_computation.13 | async-start | bytes 1474560 | tf_op jit(solution)/shard_map/reduce_scatter | solution.py:236
  138.2 11.3 collective-permute-start.1
  153.3 83.2 %all-gather.42.cloned.1.call-start = ((), (), s32[]{:S(2)}) async-start(), calls=%async_computation.29 | async-start | bytes 1474560 | tf_op jit(solution)/shard_map/all_gather | solution.py:237
  192.7 25.6 %collective-permute-start.4 = (bf16[256,768]{1,0:T(8,128)(2,1)}, bf16[256,768]{1,0:T(8,128)(2,1)}, u32[]{:S(2)}, u32[]{:S(2)}) collective-permute-start(bf16[256,768]{1,0:T(8,128)(2,1)} %add_convert_fusion.64), channel_id=1, source_target_pairs={{0,2},{1,3},{2,0},{3,1},{4,6},{5,7},{6,4},{7,5},{8,10},{9,11},{10,... | collective-permute-start | bytes 1179656 | tf_op jit(solution)/shard_map/ppermute | solution.py:257
  218.2 66.8 %all-gather.26.cloned.1.call-start = ((), (), s32[]{:S(2)}) async-start(), calls=%async_computation.14 | async-start | bytes 1966080 | tf_op jit(solution)/shard_map/all_gather | solution.py:293
  224.4 12.0 collective-permute-start.6
  247.9 144.4 %all-gather.28.cloned.1.call-start = ((), (), s32[]{:S(2)}) async-start(), calls=%async_computation.15 | async-start | bytes 1966080 | tf_op jit(solution)/shard_map/all_gather | solution.py:293
  296.4 11.2 collective-permute-start.9
  319.7 11.2 collective-permute-start.12
  333.8 12.4 collective-permute-start.14
  355.2 143.8 %all-gather.30.cloned.1.call-start = ((), (), s32[]{:S(2)}) async-start(), calls=%async_computation.16 | async-start | bytes 1966080 | tf_op jit(solution)/shard_map/all_gather | solution.py:293
  403.7 11.2 collective-permute-start.17
  429.0 11.2 collective-permute-start.20
  443.4 12.2 collective-permute-start.22
  461.9 141.9 %all-gather.32.cloned.1.call-start = ((), (), s32[]{:S(2)}) async-start(), calls=%async_computation.17 | async-start | bytes 1966080 | tf_op jit(solution)/shard_map/all_gather | solution.py:293
  510.3 11.2 collective-permute-start.25
  533.7 11.2 collective-permute-start.28
  547.8 12.0 collective-permute-start.30
  566.7 140.3 %reduce-scatter.20.cloned.1.call-start = ((), (), s32[]{:S(2)}) async-start(), calls=%async_computation.19 | async-start | bytes 1966080 | tf_op jit(solution)/shard_map/reduce_scatter | solution.py:356
  615.1 11.2 collective-permute-start.33
  640.4 11.2 collective-permute-start.39
  672.7 142.0 %reduce-scatter.22.cloned.1.call-start = ((), (), s32[]{:S(2)}) async-start(), calls=%async_computation.20 | async-start | bytes 1966080 | tf_op jit(solution)/shard_map/reduce_scatter | solution.py:356
  726.7 13.2 collective-permute-start.44
  748.6 11.2 collective-permute-start.47
  781.2 145.5 %reduce-scatter.24.cloned.1.call-start = ((), (), s32[]{:S(2)}) async-start(), calls=%async_computation.21 | async-start | bytes 1966080 | tf_op jit(solution)/shard_map/reduce_scatter | solution.py:356
  821.1 11.2 collective-permute-start.50
  836.4 13.2 collective-permute-start.52
  858.3 11.2 collective-permute-start.55
  893.1 146.8 %reduce-scatter.26.cloned.1.call-start = ((), (), s32[]{:S(2)}) async-start(), calls=%async_computation.22 | async-start | bytes 1966080 | tf_op jit(solution)/shard_map/reduce_scatter | solution.py:356
  949.5 13.2 collective-permute-start.60
  1006.4 147.2 %reduce-scatter.28.cloned.1.call-start = ((), (), s32[]{:S(2)}) async-start(), calls=%async_computation.23 | async-start | bytes 1966080 | tf_op jit(solution)/shard_map/reduce_scatter | solution.py:356
  1059.8 13.2 collective-permute-start.68
  1080.3 11.5 collective-permute-start.71
  1096.3 24.0 %collective-permute-start.35 = (bf16[256,768]{1,0:T(8,128)(2,1)}, bf16[256,768]{1,0:T(8,128)(2,1)}, u32[]{:S(2)}, u32[]{:S(2)}) collective-permute-start(bf16[256,768]{1,0:T(8,128)(2,1)} %broadcast_select_fusion.21), channel_id=1, source_target_pairs={{0,1},{1,0},{2,3},{3,2},{4,5},{5,4},{6,7},{7,6},{8,9},{9,8},{10,11... | collective-permute-start | bytes 1179656 | tf_op jit(solution)/shard_map/ppermute | solution.py:257
  1120.0 80.7 %all-gather.44.cloned.1.call-start = ((), (), s32[]{:S(2)}) async-start(), calls=%async_computation.30 | async-start | bytes 2621440 | tf_op jit(solution)/shard_map/all_gather | solution.py:243
  1122.4 11.8 collective-permute-start.36
  1146.0 158.4 %all-gather.34.cloned.1.call-start = ((), (), s32[]{:S(2)}) async-start(), calls=%async_computation.18 | async-start | bytes 3932160 | tf_op jit(solution)/shard_map/all_gather | solution.py:247
  1163.6 42.8 %collective-permute-start.74 = (bf16[256,768]{1,0:T(8,128)(2,1)}, bf16[256,768]{1,0:T(8,128)(2,1)}, u32[]{:S(2)}, u32[]{:S(2)}) collective-permute-start(bf16[256,768]{1,0:T(8,128)(2,1)} %add_convert_fusion.28), channel_id=1, source_target_pairs={{0,2},{1,3},{2,0},{3,1},{4,6},{5,7},{6,4},{7,5},{8,10},{9,11},{10,... | collective-permute-start | bytes 1179656 | tf_op jit(solution)/shard_map/ppermute | solution.py:257
  1205.9 124.5 %all-gather.46.cloned.1.call-start = ((), (), s32[]{:S(2)}) async-start(), calls=%async_computation.31 | async-start | bytes 1966080 | tf_op jit(solution)/shard_map/all_gather | solution.py:243
  1235.3 105.4 %reduce-scatter.36.cloned.1.call-start = ((), (), s32[]{:S(2)}) async-start(), calls=%async_computation.33 | async-start | bytes 491520
  1246.7 95.7 %reduce-scatter.32.cloned.1.call-start = ((), (), s32[]{:S(2)}) async-start(), calls=%async_computation.26 | async-start | bytes 1474560 | tf_op jit(solution)/shard_map/reduce_scatter | solution.py:444
  1253.8 99.9 %reduce-scatter.30.cloned.1.call-start = ((), (), s32[]{:S(2)}) async-start(), calls=%async_computation.25 | async-start | bytes 1474560 | tf_op jit(solution)/shard_map/reduce_scatter | solution.py:444
  1269.8 139.9 %reduce-scatter.34.cloned.1.call-start = ((), (), s32[]{:S(2)}) async-start(), calls=%async_computation.32 | async-start | bytes 1228800
  1286.5 131.0 %all-gather.36.cloned.1.call-start = ((), (), s32[]{:S(2)}) async-start(), calls=%async_computation.24 | async-start | bytes 2949120 | tf_op jit(solution)/shard_map/all_gather | solution.py:247
  (555 other events, 7956.8 us)
Sparse Core Ops, SparseCore 0:
  24.3 23.4 reduce-scatter.15
  79.2 44.9 all-gather.23
  125.8 30.6 all-gather.37
  158.0 29.5 all-gather.39
  189.9 28.2 reduce-scatter.17
  219.7 16.1 all-gather.41
  248.1 36.9 all-gather.25
  355.3 36.9 all-gather.27
  462.0 36.9 all-gather.29
  566.8 36.9 all-gather.31
  672.8 34.1 reduce-scatter.19
  781.3 33.3 reduce-scatter.21
  893.2 33.3 reduce-scatter.23
  1006.5 33.3 reduce-scatter.25
  1120.1 33.5 reduce-scatter.27
  1155.7 44.8 all-gather.43
  1206.1 27.2 all-gather.33
  1235.4 36.5 all-gather.45
  1274.4 19.4 reduce-scatter.35
  1296.0 27.4 reduce-scatter.31
  1325.8 27.8 reduce-scatter.29
  1356.1 25.1 reduce-scatter.33
  1383.5 25.4 all-gather.35
